TPU v7x, 512 devices: a whole 4x4x16 slice. The times are simulated.
512 devices in a mesh: blk: 128 (over z, x_hi, y), feat: 4 (over x_lo, core).
Axes of the slice: x: 4 (x_hi: 2, x_lo: 2; x = x_hi * 2 + x_lo), y: 4, z: 16, core: 2. Of those that a mesh axis runs over, the one named last changes fastest.
Arguments:
- layer_inputs: bfloat16 [1024, 2304], P('blk', 'feat'), may hold values from -6 to 6
- mlp_targets: bfloat16 [1024, 2304], P('blk', 'feat'), may hold values from -6 to 6
- enc_weight: bfloat16 [65536, 2304], P('blk', 'feat'), may hold values from -0.125 to 0.125
- enc_bias: float32 [65536], P('blk'), may hold values from -3 to 3
- act_mask: int32 [65536, 256], P('blk'), may hold values 0 or 1
- dec_weight: bfloat16 [163840, 2304], P('blk', 'feat'), may hold values from -0.046875 to 0.046875
- owner_half: int32 [128], P('blk'), may hold values from 0 to 1, as said below
Outputs:
- reconstruction: bfloat16 [1024, 2304], P('blk', 'feat')
- enc_grad: bfloat16 [65536, 2304], P('blk', 'feat')
- bias_grad: float32 [65536], P('blk')
- dec_grad: bfloat16 [163840, 2304], P('blk', 'feat')
Inputs may be any that keep to these rules, and one draw needn't show every extreme that they name: owner_half[s * 32 + g] + owner_half[(3 - s) * 32 + g] = 1 for every layer s and position g.
All inputs are finite; a program needn't handle non-finite values. No bound on the sum of `act_mask` on one device may be relied on, other than what follows from the above.
Results may differ from a plain program's by a relative error of at most 0.012.
Values may be sent and summed in bfloat16 or wider, within the bound.
No kernel may reach another device: no remote copies, remote signals or barrier semaphores. Data moves between devices by JAX's collectives and lax.ppermute only.
A program may use at most 64 MiB of HBM per device.

v0:
```python
import jax
import jax.numpy as jnp
from jax import lax
from jax.sharding import PartitionSpec as P

LAYERS = 4


def swapped(block, axis, stride):
    count = lax.axis_size(axis)
    route = []
    for low in range(count):
        high = low | 1 << stride
        if high != low and high < count:
            route += [(low, high), (high, low)]
    return lax.ppermute(block, axis, route)


def feature_total(partial_terms):
    return lax.psum(partial_terms, "feat")


def all_rows(local_rows):
    return lax.all_gather(local_rows, "blk", axis=0, tiled=True)


def swap_bits():
    total_bits = lax.axis_size("blk").bit_length() - 1
    low_bits = (lax.axis_size("blk") // LAYERS).bit_length() - 1
    return range(low_bits, total_bits)


def partner_codes(code_piece):
    for bit_number in swap_bits():
        code_piece = swapped(code_piece, "blk", bit_number)
    return code_piece


def partner_terms(term_piece):
    for bit_number in swap_bits():
        term_piece = swapped(term_piece.astype(jnp.bfloat16), "blk", bit_number).astype(
            term_piece.dtype
        )
    return term_piece


def body(layer_inputs, mlp_targets, enc_weight, enc_bias, act_mask, dec_weight, owner_half):
    group_size = lax.axis_size("blk") // LAYERS
    position = lax.axis_index("blk")
    source_layer = position // group_size
    owner_side = owner_half[0]
    width_cols = layer_inputs.shape[1]
    tokens = act_mask.shape[1]
    span_rows = enc_weight.shape[0] // 2
    slot_count = LAYERS + 1
    inputs_all = all_rows(layer_inputs)
    own_inputs = lax.dynamic_slice_in_dim(inputs_all, source_layer * tokens, tokens, 0)
    pre_part = jnp.einsum("fd,md->fm", enc_weight, own_inputs, preferred_element_type=jnp.float32)
    pre_acts = feature_total(pre_part) + enc_bias[:, None]
    mask_values = act_mask.astype(jnp.float32)
    code_block = (mask_values * pre_acts).astype(jnp.bfloat16)
    own_half = lax.dynamic_slice_in_dim(code_block, owner_side * span_rows, span_rows, 0)
    sent_half = lax.dynamic_slice_in_dim(code_block, (1 - owner_side) * span_rows, span_rows, 0)
    received = partner_codes(sent_half)
    slot_ids = jnp.arange(slot_count)
    own_slot = slot_ids < LAYERS - source_layer
    slot_target = jnp.where(own_slot, source_layer + slot_ids, slot_ids - 1)
    slot_codes = jnp.where(own_slot[:, None, None], own_half[None], received[None])
    dec_slots = dec_weight.reshape(slot_count, span_rows, width_cols)
    products = jnp.einsum("jrm,jrd->jmd", slot_codes, dec_slots, preferred_element_type=jnp.float32)
    target_hot = (slot_target[None, :] == jnp.arange(LAYERS)[:, None]).astype(jnp.float32)
    recon_part = jnp.einsum("tj,jmd->tmd", target_hot, products, precision=lax.Precision.HIGHEST)
    recon_part = recon_part.reshape(LAYERS * tokens, width_cols)
    recon_rows = lax.psum_scatter(recon_part, "blk", scatter_dimension=0, tiled=True)
    error_rows = recon_rows - mlp_targets.astype(jnp.float32)
    error_grad = all_rows(error_rows.astype(jnp.bfloat16))
    slot_grads = jnp.take(error_grad.reshape(LAYERS, tokens, width_cols), slot_target, axis=0)
    dec_grad = jnp.einsum(
        "jrm,jmd->jrd", slot_codes, slot_grads, preferred_element_type=jnp.float32
    )
    code_terms = jnp.einsum(
        "jrd,jmd->jrm", dec_slots, slot_grads, preferred_element_type=jnp.float32
    )
    own_terms = jnp.sum(jnp.where(own_slot[:, None, None], code_terms, 0.0), axis=0)
    other_terms = jnp.sum(jnp.where(own_slot[:, None, None], 0.0, code_terms), axis=0)
    returned = partner_terms(other_terms)
    first_half = jnp.where(owner_side == 0, own_terms, returned)
    second_half = jnp.where(owner_side == 0, returned, own_terms)
    code_grad = feature_total(jnp.concatenate([first_half, second_half], axis=0))
    pre_grad = mask_values * code_grad
    bias_grad = jnp.sum(pre_grad, axis=1)
    enc_grad = jnp.einsum(
        "fm,md->fd", pre_grad.astype(jnp.bfloat16), own_inputs, preferred_element_type=jnp.float32
    )
    dec_out = dec_grad.reshape(slot_count * span_rows, width_cols).astype(jnp.bfloat16)
    return (recon_rows.astype(jnp.bfloat16), enc_grad.astype(jnp.bfloat16), bias_grad, dec_out)


def solution(mesh):
    in_specs = (
        P("blk", "feat"),
        P("blk", "feat"),
        P("blk", "feat"),
        P("blk"),
        P("blk", None),
        P("blk", "feat"),
        P("blk"),
    )
    out_specs = (P("blk", "feat"), P("blk", "feat"), P("blk"), P("blk", "feat"))
    return jax.shard_map(body, mesh=mesh, in_specs=in_specs, out_specs=out_specs, check_vma=False)
```

profile of v0, /device:TPU:1, one launch (start us, length us, event | category | flops | bytes accessed | tf_op | source)
XLA Modules:
  0.0 1973.7 jit_solution(14362955889750820321)
XLA Ops:
  8.0 196.4 %all-gather.3.cloned.1.call-done = bf16[1024,576]{1,0:T(8,128)(2,1)} async-done(((bf16[8,576]{1,0:T(8,128)(2,1)}), bf16[1024,576]{1,0:T(8,128)(2,1)}) %all-gather.3.cloned.1.call-update) | async-done | bytes 1179664 | tf_op jit(solution)/shard_map/all_gather | solution.py:24
  204.4 2.1 convolution_bitcast_fusion
  207.5 58.0 %all-reduce.5.cloned.1.call-done = f32[512,256]{0,1:T(8,128)} async-done(((f32[512,256]{0,1:T(8,128)}), f32[512,256]{0,1:T(8,128)}) %all-reduce.5.cloned.1.call-update) | async-done | bytes 524304 | tf_op jit(solution)/shard_map/psum | solution.py:20
  266.8 7.0 collective-permute-start
  273.8 12.3 collective-permute-done
  286.1 12.4 collective-permute-start.1
  298.5 1.9 copy.39
  300.6 9.7 collective-permute-done.1
  311.1 3.9 fusion
  315.0 2.7 copy.50
  319.7 1277.3 %all-reduce.9.cloned.1.call-done = f32[1024,576]{1,0:T(8,128)} async-done(((f32[1024,576]{1,0:T(8,128)}), f32[1024,576]{1,0:T(8,128)}) %all-reduce.9.cloned.1.call-update) | async-done | bytes 2359312
  1598.4 264.1 %all-gather.5.cloned.1.call-done = bf16[1024,576]{1,0:T(8,128)(2,1)} async-done(((bf16[8,576]{1,0:T(8,128)(2,1)}), bf16[1024,576]{1,0:T(8,128)(2,1)}) %all-gather.5.cloned.1.call-update) | async-done | bytes 1179664 | tf_op jit(solution)/shard_map/all_gather | solution.py:24
  1862.5 1.6 copy.44
  1864.1 1.8 gather_fusion
  1866.0 2.8 select_reduce_fusion.1
  1868.8 5.4 collective-permute-start.2
  1874.1 8.6 collective-permute-done.2
  1882.7 6.5 collective-permute-start.3
  1889.3 11.9 collective-permute-done.3
  1903.4 1.8 convolution_convert_fusion
  1905.2 1.9 copy.46
  1907.1 1.6 copy.47
  1908.7 55.4 %all-reduce.7.cloned.1.call-done = f32[512,256]{0,1:T(8,128)} async-done(((f32[512,256]{0,1:T(8,128)}), f32[512,256]{0,1:T(8,128)}) %all-reduce.7.cloned.1.call-update) | async-done | bytes 524304 | tf_op jit(solution)/shard_map/psum | solution.py:20
  1964.1 2.4 convolution_convert_fusion.1
  (48 shorter events, 8.8 us)
Async XLA Ops:
  7.2 197.3 %copy-start = (bf16[512,576]{0,1:T(8,128)(2,1)S(1)}, bf16[512,576]{0,1:T(8,128)(2,1)}, u32[]{:S(2)}) copy-start(bf16[512,576]{0,1:T(8,128)(2,1)} %param.9) | copy-start | bytes 1769476
  7.2 200.1 %copy-start.8 = (s32[512,256]{1,0:T(8,128)S(1)}, s32[512,256]{1,0:T(8,128)}, u32[]{:S(2)}) copy-start(s32[512,256]{1,0:T(8,128)} %param.11) | copy-start | bytes 1572868
  7.2 197.2 %all-gather.3.cloned.1.call-start = ((), (), s32[]{:S(2)}) async-start(), calls=%async_computation | async-start | bytes 1320960 | tf_op jit(solution)/shard_map/all_gather | solution.py:24
  7.9 257.6 %all-reduce.5.cloned.1.call-start = ((), (), s32[]{:S(2)}) async-start(), calls=%async_computation.1 | async-start | bytes 1048576 | tf_op jit(solution)/shard_map/psum | solution.py:20
  8.0 257.6 %copy-start.10 = (f32[512]{0:T(512)S(1)}, f32[512]{0:T(512)}, u32[]{:S(2)}) copy-start(f32[512]{0:T(512)} %param.10) | copy-start | bytes 6148
  206.6 1390.4 %all-reduce.9.cloned.1.call-start = ((), (), s32[]{:S(2)}) async-start(), calls=%async_computation.4 | async-start | bytes 5242880
  266.8 19.4 collective-permute-start
  286.1 24.1 %collective-permute-start.1 = (bf16[256,256]{0,1:T(8,128)(2,1)S(1)}, bf16[256,256]{0,1:T(8,128)(2,1)S(1)}, u32[]{:S(2)}, u32[]{:S(2)}) collective-permute-start(bf16[256,256]{0,1:T(8,128)(2,1)S(1)} %collective-permute-done), channel_id=1, source_target_pairs={{0,256},{256,0},{4,260},{260,4},{8,264},{264,8},{12,268},{268,12},... | collective-permute-start | bytes 393224 | tf_op jit(solution)/shard_map/ppermute | solution.py:16
  300.4 10.6 copy-start.1
  300.6 10.5 copy-start.4
  310.3 0.8 copy-start.6
  317.7 1279.3 %copy-start.9 = (bf16[8,576]{1,0:T(8,128)(2,1)S(1)}, bf16[8,576]{1,0:T(8,128)(2,1)}, u32[]{:S(2)}) copy-start(bf16[8,576]{1,0:T(8,128)(2,1)} %param.8) | copy-start | bytes 27652
  317.8 1544.8 %all-gather.5.cloned.1.call-start = ((), (), s32[]{:S(2)}) async-start(), calls=%async_computation.2 | async-start | bytes 1320960 | tf_op jit(solution)/shard_map/all_gather | solution.py:24
  1598.4 365.8 %all-reduce.7.cloned.1.call-start = ((), (), s32[]{:S(2)}) async-start(), calls=%async_computation.3 | async-start | bytes 1048576 | tf_op jit(solution)/shard_map/psum | solution.py:20
  1868.7 34.7 %copy-start.3 = (bf16[5,256,576]{1,2,0:T(8,128)(2,1)S(1)}, bf16[5,256,576]{1,2,0:T(8,128)(2,1)}, u32[]{:S(2)}) copy-start(bf16[5,256,576]{1,2,0:T(8,128)(2,1)} %gather_fusion) | copy-start | bytes 4423684
  1868.8 34.7 %copy-start.5 = (bf16[256,256]{1,0:T(8,128)(2,1)S(1)}, bf16[256,256]{1,0:T(8,128)(2,1)}, u32[]{:S(2)}) copy-start(bf16[256,256]{1,0:T(8,128)(2,1)} %copy-done.4) | copy-start | bytes 393220
  1868.8 34.7 %copy-start.7 = (bf16[256,256]{1,0:T(8,128)(2,1)S(1)}, bf16[256,256]{1,0:T(8,128)(2,1)}, u32[]{:S(2)}) copy-start(bf16[256,256]{1,0:T(8,128)(2,1)} %copy-done.6) | copy-start | bytes 393220
  1868.8 14.0 collective-permute-start.2
  1882.7 18.4 collective-permute-start.3
  1964.1 2.4 copy-start.2
Sparse Core Ops, SparseCore 0:
  12.3 192.0 all-gather.2
  207.9 57.5 all-reduce.4
  317.9 1279.0 all-reduce.8
  1602.5 260.0 all-gather.4
  1902.2 61.8 all-reduce.6
where the time goes:
time: 1970 us
  waiting for transfers between devices  1890 us (96%)
  starting transfers between devices  31.5 us (2%)
    unnamed x6, waiting for transfers between devices  1280 us
    all_gather x2, waiting for transfers between devices, all_rows(): return lax.all_gather(local_rows, 'blk', axis=0, tiled=True)  461 us
    psum x2, waiting for transfers between devices, feature_total(): return lax.psum(partial_terms, 'feat')  113 us
    ppermute x4, waiting for transfers between devices, swapped(): return lax.ppermute(block, axis, route)  42.5 us
  transfers between devices with their start and end apart: 9, of which 9 were waited for; matrix products, arithmetic and copies ran while one was open for 1% of the time, Pallas kernels for 0%

commit v1 on v0

v1 whole, which is shorter than its diff:
```python
import jax
import jax.numpy as jnp
from jax import lax
from jax.sharding import Mesh, PartitionSpec as P

LAYERS = 4
BF = jnp.bfloat16
F32 = jnp.float32
AXES = ("zh", "zl", "xh", "y", "xl", "core")
FEAT = ("xl", "core")
BLK = ("zh", "zl", "xh", "y")


def exchange(pieces, axes):
    return lax.all_to_all(pieces, axes, 0, 0, tiled=True)


def share(piece, axes):
    count = lax.axis_size(axes)
    return exchange(jnp.broadcast_to(piece[None], (count,) + piece.shape), axes)


def mirror(piece):
    return lax.ppermute(piece, "zh", [(s, LAYERS - 1 - s) for s in range(LAYERS)])


def body(layer_inputs, mlp_targets, enc_weight, enc_bias, act_mask, dec_weight, owner_half):
    source = lax.axis_index("zh")
    side = owner_half[0]
    width = layer_inputs.shape[1]
    feats = enc_weight.shape[0]
    tokens = act_mask.shape[1]
    span = feats // 2
    parts = lax.axis_size(FEAT)
    quarter = span // parts
    part = lax.axis_index(FEAT)
    rows = layer_inputs.shape[0]
    zl, xy, zs = lax.axis_size("zl"), lax.axis_size(("xh", "y")), lax.axis_size(("zh", "zl"))

    own_inputs = share(layer_inputs, ("zl", "xh", "y")).reshape(tokens, width)
    pre_part = jnp.einsum("fd,md->fm", enc_weight, own_inputs, preferred_element_type=F32)
    pre_part = pre_part.astype(BF).reshape(2, parts, quarter, tokens).transpose(1, 0, 2, 3)
    pre = jnp.sum(exchange(pre_part, FEAT).astype(F32), axis=0)
    bias_q = lax.dynamic_index_in_dim(enc_bias.reshape(2, parts, quarter), part, 1, False)
    mask_q = lax.dynamic_index_in_dim(
        act_mask.reshape(2, parts, quarter, tokens), part, 1, False
    ).astype(F32)
    code_q = (mask_q * (pre + bias_q[:, :, None])).astype(BF)
    own_q = lax.dynamic_index_in_dim(code_q, side, 0, False)
    sent_q = lax.dynamic_index_in_dim(code_q, 1 - side, 0, False)
    both_q = jnp.stack([own_q, mirror(sent_q)])
    both = lax.all_gather(both_q, FEAT, axis=0)
    codes = both.transpose(1, 0, 2, 3).reshape(2, span, tokens)

    dec = dec_weight.reshape(LAYERS + 1, span, width)
    targets = jnp.arange(LAYERS)
    own_ok = targets >= source
    other_ok = targets >= LAYERS - 1 - source
    own_slot = jnp.where(own_ok, targets - source, 0)
    own_dec = jnp.take(dec, own_slot, axis=0)
    other_dec = dec[1:]
    own_codes = jnp.where(own_ok[:, None, None], codes[0][None], 0)
    other_codes = jnp.where(other_ok[:, None, None], codes[1][None], 0)
    pair_codes = jnp.concatenate([own_codes, other_codes], axis=1)
    pair_dec = jnp.concatenate([own_dec, other_dec], axis=1)
    recon_part = jnp.einsum("trm,trd->tmd", pair_codes, pair_dec, preferred_element_type=F32)
    pieces = recon_part.astype(BF).reshape(zs, xy, rows, width).transpose(1, 0, 2, 3)
    sums = jnp.sum(exchange(pieces, ("xh", "y")).astype(F32), axis=0).astype(BF)
    recon_rows = jnp.sum(exchange(sums, ("zh", "zl")).astype(F32), axis=0)
    error_rows = (recon_rows - mlp_targets.astype(F32)).astype(BF)
    error_z = share(error_rows, ("zh", "zl"))
    error = share(error_z, ("xh", "y"))
    error = error.transpose(1, 0, 2, 3).reshape(LAYERS, tokens, width)

    err_own = jnp.where(own_ok[:, None, None], error, 0)
    err_other = jnp.where(other_ok[:, None, None], error, 0)
    own_terms = jnp.einsum("trd,tmd->rm", own_dec, err_own, preferred_element_type=F32)
    other_terms = jnp.einsum("trd,tmd->rm", other_dec, err_other, preferred_element_type=F32)
    terms = jnp.stack([own_terms, other_terms]).astype(BF)
    terms = terms.reshape(2, parts, quarter, tokens).transpose(1, 0, 2, 3)
    terms_q = jnp.sum(exchange(terms, FEAT).astype(F32), axis=0)
    returned = mirror(terms_q[1].astype(BF)).astype(F32)
    grad_q = jnp.where(side == 0, jnp.stack([terms_q[0], returned]), jnp.stack([returned, terms_q[0]]))
    pre_grad_q = (mask_q * grad_q).astype(BF)
    pre_grad = lax.all_gather(pre_grad_q, FEAT, axis=0)
    pre_grad = pre_grad.transpose(1, 0, 2, 3).reshape(feats, tokens)
    bias_grad = jnp.sum(pre_grad.astype(F32), axis=1)
    enc_grad = jnp.einsum("fm,md->fd", pre_grad, own_inputs, preferred_element_type=F32)

    slots = jnp.arange(LAYERS + 1)
    slot_own = slots < LAYERS - source
    slot_target = jnp.where(slot_own, source + slots, slots - 1)
    slot_codes = jnp.where(slot_own[:, None, None], codes[0][None], codes[1][None])
    slot_err = jnp.take(error, slot_target, axis=0)
    dec_grad = jnp.einsum("jrm,jmd->jrd", slot_codes, slot_err, preferred_element_type=F32)
    dec_out = dec_grad.astype(BF).reshape(dec_weight.shape)
    return (recon_rows.astype(BF), enc_grad.astype(BF), bias_grad, dec_out)


def solution(mesh):
    fine = Mesh(mesh.devices.reshape(LAYERS, 4, 2, 4, 2, 2), AXES)
    wide = P(BLK, FEAT)
    in_specs = (wide, wide, wide, P(BLK), P(BLK, None), wide, P(BLK))
    out_specs = (wide, wide, P(BLK), wide)
    return jax.shard_map(body, mesh=fine, in_specs=in_specs, out_specs=out_specs, check_vma=False)
```

time: 1970 us -> 189 us (0.10)
  waiting for transfers between devices: 1890 us -> 22.5 us
  blocking collectives: 0 us -> 76.7 us
    unnamed x6 -> x0, waiting for transfers between devices: 1280 us -> none
    all_gather x2 -> x0, waiting for transfers between devices: 461 us -> none  [all_rows(): return lax.all_gather(local_rows, 'blk', axis=0, tiled=True)]
    psum x2 -> x0, waiting for transfers between devices: 113 us -> none  [feature_total(): return lax.psum(partial_terms, 'feat')]
    all_to_all x0 -> x3, blocking collectives: none -> 61.7 us  [exchange(): return lax.all_to_all(pieces, axes, 0, 0, tiled=True)]
    ppermute x4 -> x2, waiting for transfers between devices: 42.5 us -> 3.79 us  [mirror(): lax.ppermute(piece, 'zh', [(s, LAYERS - 1 - s) for s in range(LAYERS)])]
    all_to_all x0 -> x4, starting transfers between devices: none -> 34.8 us  [exchange(): return lax.all_to_all(pieces, axes, 0, 0, tiled=True)]
  transfers between devices with their start and end apart: 9 -> 6, of which waited for: 9 -> 5; matrix products, arithmetic and copies ran while one was open for 1% -> 9% of each run, Pallas kernels for 0% -> 0%
where the time goes in v1:
time: 189 us; the launch traced here: 188 us
  blocking collectives  76.7 us (41%)
  starting transfers between devices  50.3 us (27%)
  waiting for transfers between devices  22.5 us (12%)
  local copies, waits for them, and re-layouts  21.2 us (11%)
  matrix products  8.61 us (5%)
  other arithmetic  6.71 us (4%)
    all_to_all x3, blocking collectives, exchange(): return lax.all_to_all(pieces, axes, 0, 0, tiled=True)  61.7 us
    all_to_all x4, starting transfers between devices, exchange(): return lax.all_to_all(pieces, axes, 0, 0, tiled=True)  34.8 us
    all_to_all x4, waiting for transfers between devices, exchange(): return lax.all_to_all(pieces, axes, 0, 0, tiled=True)  18.7 us
    ppermute x2, starting transfers between devices, mirror(): lax.ppermute(piece, 'zh', [(s, LAYERS - 1 - s) for s in range(LAYERS)])  15.5 us
    all_gather x1, blocking collectives, body(): pre_grad = lax.all_gather(pre_grad_q, FEAT, axis=0)  7.49 us
    all_gather x1, blocking collectives, body(): both = lax.all_gather(both_q, FEAT, axis=0)  7.44 us
    unnamed x30, local copies, waits for them, and re-layouts  5.26 us
    ppermute x2, waiting for transfers between devices, mirror(): lax.ppermute(piece, 'zh', [(s, LAYERS - 1 - s) for s in range(LAYERS)])  3.79 us
  transfers between devices with their start and end apart: 6, of which 5 were waited for; matrix products, arithmetic and copies ran while one was open for 9% of the time, Pallas kernels for 0%

profile of v1, /device:TPU:1, one launch (start us, length us, event | category | flops | bytes accessed | tf_op | source)
XLA Modules:
  0.0 187.5 jit_solution(9416049859153927198)
XLA Ops:
  2.2 11.9 %all-to-all-start = ((bf16[32,8,576]{2,1,0:T(8,128)(2,1)}), bf16[32,8,576]{2,1,0:T(8,128)(2,1)S(1)}, u32[]{:S(2)}, u32[]{:S(2)}) async-start(bf16[32,8,576]{2,1,0:T(8,128)(2,1)} %broadcast_in_dim.128), calls=%async_computation | async-start | bytes 655360 | tf_op jit(solution)/shard_map/all_to_all | solution.py:15
  14.1 1.9 %copy.73 = bf16[1280,576]{1,0:T(8,128)(2,1)S(1)} copy(bf16[1280,576]{0,1:T(8,128)(2,1)} %param.12) | data formatting | bytes 2949120 | tf_op args[5]
  17.6 2.0 %gather_fusion = bf16[4,256,576]{1,2,0:T(8,128)(2,1)S(1)} fusion(bf16[5,256,576]{1,2,0:T(8,128)(2,1)} %copy.74, s32[1024]{0:T(1024)S(1)} %pad_clamp_fusion.1), kind=kCustom, calls=%fused_computation | custom fusion | bytes 2359312 | tf_op jit(solution)/shard_map/jit(_take)/gather | solution.py:60
  19.7 5.8 %all-to-all-done = bf16[32,8,576]{2,1,0:T(8,128)(2,1)S(1)} async-done(((bf16[32,8,576]{2,1,0:T(8,128)(2,1)}), bf16[32,8,576]{2,1,0:T(8,128)(2,1)S(1)}, u32[]{:S(2)}, u32[]{:S(2)}) %all-to-all-start) | async-done | bytes 294944 | tf_op jit(solution)/shard_map/all_to_all | solution.py:15
  26.6 7.2 %all-to-all-start.1 = ((bf16[4,2,64,256]{3,2,1,0:T(8,128)(2,1)}), bf16[4,2,64,256]{3,2,1,0:T(8,128)(2,1)S(1)}, u32[]{:S(2)}, u32[]{:S(2)}) async-start(bf16[4,2,64,256]{3,2,1,0:T(8,128)(2,1)} %bitcast.86), calls=%async_computation.1 | async-start | bytes 524288 | tf_op jit(solution)/shard_map/all_to_all | solution.py:15
  35.8 3.2 %all-to-all-done.1 = bf16[4,2,64,256]{3,2,1,0:T(8,128)(2,1)S(1)} async-done(((bf16[4,2,64,256]{3,2,1,0:T(8,128)(2,1)}), bf16[4,2,64,256]{3,2,1,0:T(8,128)(2,1)S(1)}, u32[]{:S(2)}, u32[]{:S(2)}) %all-to-all-start.1) | async-done | bytes 262176 | tf_op jit(solution)/shard_map/all_to_all | solution.py:15
  40.0 9.8 %collective-permute-start = (bf16[64,256]{1,0:T(8,128)(2,1)S(1)}, bf16[64,256]{1,0:T(8,128)(2,1)S(1)}, u32[]{:S(2)}, u32[]{:S(2)}) collective-permute-start(bf16[64,256]{1,0:T(8,128)(2,1)S(1)} %get-tuple-element.27), channel_id=1, source_target_pairs={{0,384},{128,256},{256,128},{384,0},{1,385},{129,257},{257,129},{3... | collective-permute-start | bytes 98312 | tf_op jit(solution)/shard_map/ppermute | solution.py:24
  51.1 7.4 %all-gather = bf16[8,64,256]{2,1,0:T(8,128)(2,1)S(1)} all-gather(bf16[2,64,256]{2,1,0:T(8,128)(2,1)S(1)} %pad_maximum_fusion), channel_id=2, replica_groups=mesh['zh'=4,'zl'=4,'xh'=2,'y'=4,'xl'=2,'core'=2] {'xl','core'}, dimensions={0}, use_global_device_ids=true | all-gather | bytes 327680 | tf_op jit(solution)/shard_map/all_gather | solution.py:52
  59.4 1.8 fusion.6
  61.2 1.7 copy.76
  63.0 21.4 %all_to_all.35 = bf16[8,16,8,576]{3,2,1,0:T(8,128)(2,1)S(1)} all-to-all(bf16[8,16,8,576]{3,2,1,0:T(8,128)(2,1)S(1)} %copy.77), channel_id=1, replica_groups=mesh['zh'=4,'zl'=4,'xh'=2,'y'=4,'xl'=2,'core'=2] {'xh','y'}, dimensions={0} | all-to-all | bytes 2359296 | tf_op jit(solution)/shard_map/all_to_all | solution.py:15
  84.7 21.9 %all_to_all.36 = bf16[16,8,576]{2,1,0:T(8,128)(2,1)S(1)} all-to-all(bf16[16,8,576]{2,1,0:T(8,128)(2,1)S(1)} %reduce_sum.51), channel_id=1, replica_groups=mesh['zh'=4,'zl'=4,'xh'=2,'y'=4,'xl'=2,'core'=2] {'zh','zl'}, dimensions={0} | all-to-all | bytes 294912 | tf_op jit(solution)/shard_map/all_to_all | solution.py:15
  107.2 18.4 %all_to_all.37 = bf16[16,8,576]{2,1,0:T(8,128)(2,1)S(1)} all-to-all(bf16[16,8,576]{2,1,0:T(8,128)(2,1)S(1)} %broadcast_in_dim.140), channel_id=1, replica_groups=mesh['zh'=4,'zl'=4,'xh'=2,'y'=4,'xl'=2,'core'=2] {'zh','zl'}, dimensions={0} | all-to-all | bytes 294912 | tf_op jit(solution)/shard_map/all_to_all | solution.py:15
  126.8 5.4 %all-to-all-start.5 = ((bf16[8,16,8,576]{3,2,1,0:T(8,128)(2,1)}), bf16[8,16,8,576]{3,2,1,0:T(8,128)(2,1)S(1)}, u32[]{:S(2)}, u32[]{:S(2)}) async-start(bf16[8,16,8,576]{3,2,1,0:T(8,128)(2,1)} %broadcast_in_dim.141), calls=%async_computation.5 | async-start | bytes 2621440 | tf_op jit(solution)/shard_map/all_to_all | solution.py:15
  133.4 2.4 %copy.78 = bf16[256,576,4]{1,0,2:T(8,128)(2,1)} copy(bf16[256,576,4]{0,1,2:T(8,128)(2,1)} %fusion.57) | data formatting | bytes 2359296 | tf_op jit(solution)/shard_map/jit(_take)/select_n | solution.py:60
  135.9 9.7 %all-to-all-done.5 = bf16[8,16,8,576]{3,2,1,0:T(8,128)(2,1)S(1)} async-done(((bf16[8,16,8,576]{3,2,1,0:T(8,128)(2,1)}), bf16[8,16,8,576]{3,2,1,0:T(8,128)(2,1)S(1)}, u32[]{:S(2)}, u32[]{:S(2)}) %all-to-all-start.5) | async-done | bytes 1179680 | tf_op jit(solution)/shard_map/all_to_all | solution.py:15
  149.0 2.0 %fusion.28 = bf16[1,4,64,256]{3,2,1,0:T(8,128)(2,1)S(1)} fusion(bf16[4,64,576,4]{2,1,0,3:T(8,128)(2,1)} %bitcast.102, bf16[4,256,576]{2,1,0:T(8,128)(2,1)S(1)} %bitcast.95, pred[4]{0:T(512)(128)(4,1)S(1)} %get-tuple-element.31), kind=kOutput, calls=%fused_computation.25 | convolution fusion | flops 302645248 | bytes 2490372 | tf_op jit(solution)/shard_map/trd,tmd->rm/dot_general | solution.py:77
  151.8 10.2 %all-to-all-start.6 = ((bf16[4,2,64,256]{3,2,1,0:T(8,128)(2,1)}), bf16[4,2,64,256]{3,2,1,0:T(8,128)(2,1)}, u32[]{:S(2)}, u32[]{:S(2)}) async-start(bf16[4,2,64,256]{3,2,1,0:T(8,128)(2,1)} %copy.83), calls=%async_computation.6 | async-start | bytes 524288 | tf_op jit(solution)/shard_map/all_to_all | solution.py:15
  162.0 1.9 %convolution_convert_fusion = bf16[5,256,576]{1,2,0:T(8,128)(2,1)} fusion(bf16[5,256,576]{2,1,0:T(8,128)(2,1)S(1)} %gather_fusion.1, pred[5]{0:T(512)(128)(4,1)S(1)} %get-tuple-element.32, pred[5]{0:T(512)(128)(4,1)S(1)} %get-tuple-element.33, bf16[256,256]{1,0:T(8,128)(2,1)S(1)} %bitcast.110, bf16[256,256]{1,0:T(8,128)(2,1)S(1)} %bitcast.108), kind=kOutput, calls=%fused_computation.6 | convolution fusion | flops 379289600 | bytes 3211274 | tf_op jit(solution)/shard_map/jrm,jmd->jrd/dot_general | solution.py:95
  163.9 1.9 %copy.88 = bf16[5,256,576]{2,1,0:T(8,128)(2,1)S(1)} copy(bf16[5,256,576]{1,2,0:T(8,128)(2,1)} %convolution_convert_fusion) | data formatting | bytes 2949120 | tf_op jit(solution)/shard_map/convert_element_type | solution.py:96
  165.8 1.6 copy.89
  168.5 5.8 %collective-permute-start.1 = (bf16[64,256]{1,0:T(8,128)(2,1)S(1)}, bf16[64,256]{1,0:T(8,128)(2,1)S(1)}, u32[]{:S(2)}, u32[]{:S(2)}) collective-permute-start(bf16[64,256]{1,0:T(8,128)(2,1)S(1)} %fusion.46), channel_id=1, source_target_pairs={{0,384},{128,256},{256,128},{384,0},{1,385},{129,257},{257,129},{3... | collective-permute-start | bytes 98312 | tf_op jit(solution)/shard_map/ppermute | solution.py:24
  174.3 2.8 %collective-permute-done.1 = bf16[64,256]{1,0:T(8,128)(2,1)S(1)} collective-permute-done((bf16[64,256]{1,0:T(8,128)(2,1)S(1)}, bf16[64,256]{1,0:T(8,128)(2,1)S(1)}, u32[]{:S(2)}, u32[]{:S(2)}) %collective-permute-start.1) | collective-permute-done | bytes 32800 | tf_op jit(solution)/shard_map/ppermute | solution.py:24
  178.0 7.5 %all_gather.12 = bf16[4,2,64,256]{3,2,1,0:T(8,128)(2,1)S(1)} all-gather(bf16[1,2,64,256]{3,2,1,0:T(8,128)(2,1)S(1)} %fusion.44), channel_id=1, replica_groups=mesh['zh'=4,'zl'=4,'xh'=2,'y'=4,'xl'=2,'core'=2] {'xl','core'}, dimensions={0}, use_global_device_ids=true | all-gather | bytes 327680 | tf_op jit(solution)/shard_map/all_gather | solution.py:85
  (74 shorter events, 20.3 us)
Async XLA Ops:
  0.6 24.8 %copy-start = (bf16[512,576]{0,1:T(8,128)(2,1)S(1)}, bf16[512,576]{0,1:T(8,128)(2,1)}, u32[]{:S(2)}) copy-start(bf16[512,576]{0,1:T(8,128)(2,1)} %param.9) | copy-start | bytes 1769476
  2.2 23.3 %all-to-all-start = ((bf16[32,8,576]{2,1,0:T(8,128)(2,1)}), bf16[32,8,576]{2,1,0:T(8,128)(2,1)S(1)}, u32[]{:S(2)}, u32[]{:S(2)}) async-start(bf16[32,8,576]{2,1,0:T(8,128)(2,1)} %broadcast_in_dim.128), calls=%async_computation | async-start | bytes 655360 | tf_op jit(solution)/shard_map/all_to_all | solution.py:15
  25.4 8.4 %copy-start.4 = (bf16[32,8,576]{2,1,0:T(8,128)(2,1)}, bf16[32,8,576]{2,1,0:T(8,128)(2,1)S(1)}, u32[]{:S(2)}) copy-start(bf16[32,8,576]{2,1,0:T(8,128)(2,1)S(1)} %all-to-all-done) | copy-start | bytes 884740
  26.6 12.4 %all-to-all-start.1 = ((bf16[4,2,64,256]{3,2,1,0:T(8,128)(2,1)}), bf16[4,2,64,256]{3,2,1,0:T(8,128)(2,1)S(1)}, u32[]{:S(2)}, u32[]{:S(2)}) async-start(bf16[4,2,64,256]{3,2,1,0:T(8,128)(2,1)} %bitcast.86), calls=%async_computation.1 | async-start | bytes 524288 | tf_op jit(solution)/shard_map/all_to_all | solution.py:15
  33.8 1.2 copy-start.13
  33.8 16.0 %copy-start.1 = (bf16[1280,576]{0,1:T(8,128)(2,1)S(1)}, bf16[1280,576]{0,1:T(8,128)(2,1)}, u32[]{:S(2)}) copy-start(bf16[1280,576]{0,1:T(8,128)(2,1)} %param.12) | copy-start | bytes 4423684
  40.0 11.1 %collective-permute-start = (bf16[64,256]{1,0:T(8,128)(2,1)S(1)}, bf16[64,256]{1,0:T(8,128)(2,1)S(1)}, u32[]{:S(2)}, u32[]{:S(2)}) collective-permute-start(bf16[64,256]{1,0:T(8,128)(2,1)S(1)} %get-tuple-element.27), channel_id=1, source_target_pairs={{0,384},{128,256},{256,128},{384,0},{1,385},{129,257},{257,129},{3... | collective-permute-start | bytes 98312 | tf_op jit(solution)/shard_map/ppermute | solution.py:24
  50.0 8.6 %copy-start.2 = (bf16[1024,576]{0,1:T(8,128)(2,1)}, bf16[1024,576]{0,1:T(8,128)(2,1)S(1)}, u32[]{:S(2)}) copy-start(bf16[1024,576]{0,1:T(8,128)(2,1)S(1)} %slice.26) | copy-start | bytes 3538948
  50.1 9.3 %copy-start.6 = (bf16[4,256,576]{1,2,0:T(8,128)(2,1)S(1)}, bf16[4,256,576]{1,2,0:T(8,128)(2,1)}, u32[]{:S(2)}) copy-start(bf16[4,256,576]{1,2,0:T(8,128)(2,1)} %broadcast_select_fusion) | copy-start | bytes 3538948
  58.6 0.7 copy-start.7
  58.6 0.7 copy-start.9
  84.5 22.2 %copy-start.12 = (bf16[8,576]{1,0:T(8,128)(2,1)S(1)}, bf16[8,576]{1,0:T(8,128)(2,1)}, u32[]{:S(2)}) copy-start(bf16[8,576]{1,0:T(8,128)(2,1)} %param.8) | copy-start | bytes 27652
  126.8 18.7 %all-to-all-start.5 = ((bf16[8,16,8,576]{3,2,1,0:T(8,128)(2,1)}), bf16[8,16,8,576]{3,2,1,0:T(8,128)(2,1)S(1)}, u32[]{:S(2)}, u32[]{:S(2)}) async-start(bf16[8,16,8,576]{3,2,1,0:T(8,128)(2,1)} %broadcast_in_dim.141), calls=%async_computation.5 | async-start | bytes 2621440 | tf_op jit(solution)/shard_map/all_to_all | solution.py:15
  145.5 1.3 copy-start.3
  149.0 2.0 %copy-start.11 = (bf16[256,256]{0,1:T(8,128)(2,1)S(1)}, bf16[256,256]{0,1:T(8,128)(2,1)}, u32[]{:S(2)}) copy-start(bf16[256,256]{0,1:T(8,128)(2,1)} %fusion.25) | copy-start | bytes 393220
  151.0 11.0 %copy-start.8 = (bf16[1,4,64,256]{3,2,0,1:T(8,128)(2,1)S(1)}, bf16[1,4,64,256]{3,2,0,1:T(8,128)(2,1)}, u32[]{:S(2)}) copy-start(bf16[1,4,64,256]{3,2,0,1:T(8,128)(2,1)} %copy-done.7) | copy-start | bytes 393220
  151.0 11.0 %copy-start.10 = (bf16[1,4,64,256]{3,2,0,1:T(8,128)(2,1)S(1)}, bf16[1,4,64,256]{3,2,0,1:T(8,128)(2,1)}, u32[]{:S(2)}) copy-start(bf16[1,4,64,256]{3,2,0,1:T(8,128)(2,1)} %copy-done.9) | copy-start | bytes 393220
  151.8 15.6 %all-to-all-start.6 = ((bf16[4,2,64,256]{3,2,1,0:T(8,128)(2,1)}), bf16[4,2,64,256]{3,2,1,0:T(8,128)(2,1)}, u32[]{:S(2)}, u32[]{:S(2)}) async-start(bf16[4,2,64,256]{3,2,1,0:T(8,128)(2,1)} %copy.83), calls=%async_computation.6 | async-start | bytes 524288 | tf_op jit(solution)/shard_map/all_to_all | solution.py:15
  167.4 18.9 %copy-start.5 = (bf16[32,8,576]{2,1,0:T(8,128)(2,1)S(1)}, bf16[32,8,576]{2,1,0:T(8,128)(2,1)}, u32[]{:S(2)}) copy-start(bf16[32,8,576]{2,1,0:T(8,128)(2,1)} %copy-done.4) | copy-start | bytes 884740
  168.5 8.6 %collective-permute-start.1 = (bf16[64,256]{1,0:T(8,128)(2,1)S(1)}, bf16[64,256]{1,0:T(8,128)(2,1)S(1)}, u32[]{:S(2)}, u32[]{:S(2)}) collective-permute-start(bf16[64,256]{1,0:T(8,128)(2,1)S(1)} %fusion.46), channel_id=1, source_target_pairs={{0,384},{128,256},{256,128},{384,0},{1,385},{129,257},{257,129},{3... | collective-permute-start | bytes 98312 | tf_op jit(solution)/shard_map/ppermute | solution.py:24

commit v2 on v1

v2 whole, which is shorter than its diff:
```python
import jax
import jax.numpy as jnp
from jax import lax
from jax.experimental import pallas as pl
from jax.experimental.pallas import tpu as pltpu
from jax.sharding import Mesh, PartitionSpec as P

LAYERS = 4
BF = jnp.bfloat16
F32 = jnp.float32
AXES = ("zh", "zm", "zb", "xh", "y", "xl", "core")
NEAR = ("zb", "xh", "y")
FAR = ("zh", "zm")
FEAT = ("xl", "core")
BLK = ("zh", "zm", "zb", "xh", "y")
VMEM_BYTES = 40 * 1024 * 1024


def exchange(pieces, axes):
    return lax.all_to_all(pieces, axes, 0, 0, tiled=True)


def share(piece, axes):
    count = lax.axis_size(axes)
    return exchange(jnp.broadcast_to(piece[None], (count,) + piece.shape), axes)


def mirror(piece):
    return lax.ppermute(piece, "zh", [(s, LAYERS - 1 - s) for s in range(LAYERS)])


def own_slot(source, target):
    return pl.multiple_of(jnp.maximum(target - source, 0) * 256, 256)


def recon_kernel(source_ref, codes_ref, dec_ref, out_ref):
    source = source_ref[0]
    groups, _, rows, width = out_ref.shape
    span = codes_ref.shape[1] // 2
    for target in range(LAYERS):
        own = jnp.where(target >= source, codes_ref[:, :span], 0)
        other = jnp.where(target >= LAYERS - 1 - source, codes_ref[:, span:], 0)
        own_dec = dec_ref[:, pl.ds(own_slot(source, target), span)]
        other_dec = dec_ref[:, (target + 1) * span : (target + 2) * span]
        dims = (((1,), (1,)), ((), ()))
        total = lax.dot_general(own.astype(BF), own_dec, dims, preferred_element_type=F32)
        total += lax.dot_general(other.astype(BF), other_dec, dims, preferred_element_type=F32)
        out_ref[:, target] = total.astype(BF).reshape(groups, rows, width)


def terms_kernel(source_ref, error_ref, dec_ref, out_ref):
    source = source_ref[0]
    width = error_ref.shape[3]
    tokens, both = out_ref.shape
    span = both // 2
    own_sum = jnp.zeros((tokens, span), F32)
    other_sum = jnp.zeros((tokens, span), F32)
    for target in range(LAYERS):
        error = error_ref[:, target].reshape(tokens, width)
        own_dec = dec_ref[:, pl.ds(own_slot(source, target), span)]
        other_dec = dec_ref[:, (target + 1) * span : (target + 2) * span]
        own = jnp.dot(error, own_dec, preferred_element_type=F32)
        other = jnp.dot(error, other_dec, preferred_element_type=F32)
        own_sum += jnp.where(target >= source, own, 0.0)
        other_sum += jnp.where(target >= LAYERS - 1 - source, other, 0.0)
    out_ref[:, :span] = own_sum.astype(BF)
    out_ref[:, span:] = other_sum.astype(BF)


def dec_grad_kernel(source_ref, error_ref, codes_ref, out_ref):
    source = source_ref[0]
    width = error_ref.shape[3]
    tokens, both = codes_ref.shape
    span = both // 2
    for slot in range(LAYERS + 1):
        is_own = slot < LAYERS - source
        target = jnp.where(is_own, source + slot, slot - 1)
        error = error_ref[:, pl.ds(target, 1)].reshape(tokens, width)
        codes = jnp.where(is_own, codes_ref[:, :span], codes_ref[:, span:])
        grad = lax.dot_general(
            error, codes, (((0,), (0,)), ((), ())), preferred_element_type=F32
        )
        out_ref[:, slot * span : (slot + 1) * span] = grad.astype(BF)


def call(kernel, shape, flops, moved, *operands):
    specs = [pl.BlockSpec(memory_space=pltpu.SMEM)]
    specs += [pl.BlockSpec(memory_space=pltpu.VMEM)] * (len(operands) - 1)
    return pl.pallas_call(
        kernel,
        out_shape=jax.ShapeDtypeStruct(shape, BF),
        in_specs=specs,
        out_specs=pl.BlockSpec(memory_space=pltpu.VMEM),
        compiler_params=pltpu.CompilerParams(vmem_limit_bytes=VMEM_BYTES),
        cost_estimate=pl.CostEstimate(flops=flops, bytes_accessed=moved, transcendentals=0),
    )(*operands)


def body(layer_inputs, mlp_targets, enc_weight, enc_bias, act_mask, dec_weight, owner_half):
    source = lax.axis_index("zh").astype(jnp.int32).reshape(1)
    first = owner_half[0] == 0
    rows, width = layer_inputs.shape
    feats, tokens = act_mask.shape
    span = feats // 2
    parts = lax.axis_size(FEAT)
    near, far = lax.axis_size(NEAR), lax.axis_size(FAR)
    zm = lax.axis_size("zm")
    quarter = tokens // parts

    place = lax.axis_index(FEAT) * quarter + jnp.arange(quarter)
    token = place // rows % zm * (near * rows) + place // (rows * zm) * rows + place % rows
    picked = (token[:, None] == jnp.arange(tokens)[None, :]).astype(BF)
    mask_q = jnp.einsum("qm,fm->qf", picked, act_mask.astype(BF), preferred_element_type=F32)
    dec = dec_weight.T

    own_inputs = share(layer_inputs, NEAR + ("zm",)).reshape(tokens, width)
    pre_part = jnp.einsum("md,fd->mf", own_inputs, enc_weight, preferred_element_type=F32)
    pre_part = pre_part.astype(BF).reshape(parts, quarter, feats)
    pre = jnp.sum(exchange(pre_part, FEAT).astype(F32), axis=0) + enc_bias[None, :]
    code_q = (mask_q * pre).astype(BF)
    low, high = code_q[:, :span], code_q[:, span:]
    received = mirror(jnp.where(first, high, low))
    both_q = jnp.concatenate([jnp.where(first, low, high), received], axis=1)
    codes = lax.all_gather(both_q, FEAT, axis=0, tiled=True)

    pieces = call(
        recon_kernel, (near, LAYERS, zm * rows, width), 8 * 2 * tokens * span * width, 3000000,
        source, codes, dec,
    )
    sums = jnp.sum(exchange(pieces, NEAR).astype(F32), axis=0).astype(BF)
    sums = sums.reshape(far, rows, width)
    recon_rows = jnp.sum(exchange(sums, FAR).astype(F32), axis=0)
    error_rows = (recon_rows - mlp_targets.astype(F32)).astype(BF)
    error = share(error_rows, FAR).reshape(LAYERS, zm * rows, width)
    error = share(error, NEAR).reshape(near, LAYERS, zm * rows, width)

    terms = call(
        terms_kernel, (tokens, feats), 8 * 2 * tokens * span * width, 3000000,
        source, error, dec,
    )
    terms = exchange(terms.reshape(parts, quarter, feats), FEAT)
    terms_q = jnp.sum(terms.astype(F32), axis=0)
    returned = mirror(terms_q[:, span:].astype(BF)).astype(F32)
    own = terms_q[:, :span]
    grad_q = jnp.concatenate(
        [jnp.where(first, own, returned), jnp.where(first, returned, own)], axis=1
    )
    pre_grad = lax.all_gather((mask_q * grad_q).astype(BF), FEAT, axis=0, tiled=True)
    bias_grad = jnp.sum(pre_grad.astype(F32), axis=0)
    enc_grad = jnp.einsum("mf,md->fd", pre_grad, own_inputs, preferred_element_type=F32)
    dec_grad = call(
        dec_grad_kernel, dec.shape, 5 * 2 * tokens * span * width, 3000000,
        source, error, codes,
    )
    return (recon_rows.astype(BF), enc_grad.astype(BF), bias_grad, dec_grad.T)


def solution(mesh):
    fine = Mesh(mesh.devices.reshape(LAYERS, 2, 2, 2, 4, 2, 2), AXES)
    wide = P(BLK, FEAT)
    in_specs = (wide, wide, wide, P(BLK), P(BLK, None), wide, P(BLK))
    out_specs = (wide, wide, P(BLK), wide)
    return jax.shard_map(body, mesh=fine, in_specs=in_specs, out_specs=out_specs, check_vma=False)
```

time: 189 us -> 173 us (0.915)
  blocking collectives: 76.7 us -> 132 us
  starting transfers between devices: 50.3 us -> 17.6 us
  local copies, waits for them, and re-layouts: 21.2 us -> 0.98 us
  waiting for transfers between devices: 22.5 us -> 10.8 us
  matrix products: 8.61 us -> 2.46 us
  other arithmetic: 6.71 us -> 2.92 us
  Pallas kernels: 0 us -> 3.77 us
    all_to_all x3 -> x6, blocking collectives: 61.7 us -> 117 us  [exchange(): return lax.all_to_all(pieces, axes, 0, 0, tiled=True)]
    all_to_all x4 -> x1, starting transfers between devices: 34.8 us -> 5.77 us  [exchange(): return lax.all_to_all(pieces, axes, 0, 0, tiled=True)]
    all_to_all x4 -> x1, waiting for transfers between devices: 18.7 us -> 4.49 us  [exchange(): return lax.all_to_all(pieces, axes, 0, 0, tiled=True)]
    dot_general x6 -> x3, matrix products: 8.61 us -> 2.46 us  [the longest x1 1.17 us: body(): jnp.einsum('mf,md->fd', pre_grad, own_inputs, preferred_element_type=F32)]
    unnamed x30 -> x10, local copies, waits for them, and re-layouts: 5.26 us -> 0.03 us
    pallas_call x0 -> x3, Pallas kernels: none -> 3.77 us  [call(): pl.pallas_call(kernel, out_shape=jax.ShapeDtypeStruct(shape, BF), in_spec...]
    ppermute x2, starting transfers between devices: 15.5 us -> 11.8 us  [mirror(): lax.ppermute(piece, 'zh', [(s, LAYERS - 1 - s) for s in range(LAYERS)])]
    convert_element_type x3 -> x0, local copies, waits for them, and re-layouts: 3.56 us -> none  [the longest x1 1.88 us: body(): dec_out = dec_grad.astype(BF).reshape(dec_weight.shape)]
  transfers between devices with their start and end apart: 6 -> 3, of which waited for: 5 -> 3; matrix products, arithmetic and copies ran while one was open for 9% -> 0% of each run, Pallas kernels for 0% -> 1%
where the time goes in v2:
time: 173 us; the launch traced here: 172 us
  blocking collectives  132 us (76%)
  starting transfers between devices  17.6 us (10%)
  waiting for transfers between devices  10.8 us (6%)
  Pallas kernels  3.77 us (2%)
  other arithmetic  2.92 us (2%)
  matrix products  2.46 us (1%)
    all_to_all x6, blocking collectives, exchange(): return lax.all_to_all(pieces, axes, 0, 0, tiled=True)  117 us
    ppermute x2, starting transfers between devices, mirror(): lax.ppermute(piece, 'zh', [(s, LAYERS - 1 - s) for s in range(LAYERS)])  11.8 us
    all_gather x1, blocking collectives, body(): lax.all_gather((mask_q * grad_q).astype(BF), FEAT, axis=0, tiled=True)  7.8 us
    all_gather x1, blocking collectives, body(): codes = lax.all_gather(both_q, FEAT, axis=0, tiled=True)  7.25 us
    ppermute x2, waiting for transfers between devices, mirror(): lax.ppermute(piece, 'zh', [(s, LAYERS - 1 - s) for s in range(LAYERS)])  6.27 us
    all_to_all x1, starting transfers between devices, exchange(): return lax.all_to_all(pieces, axes, 0, 0, tiled=True)  5.77 us
    all_to_all x1, waiting for transfers between devices, exchange(): return lax.all_to_all(pieces, axes, 0, 0, tiled=True)  4.49 us
    pallas_call x3, Pallas kernels, call(): pl.pallas_call(kernel, out_shape=jax.ShapeDtypeStruct(shape, BF), in_spec...  3.77 us
  transfers between devices with their start and end apart: 3, of which 3 were waited for; matrix products, arithmetic and copies ran while one was open for 0% of the time, Pallas kernels for 1%

profile of v2, /device:TPU:1, one launch (start us, length us, event | category | flops | bytes accessed | tf_op | source)
XLA Modules:
  0.0 172.2 jit_solution(5669264679630467792)
XLA Ops:
  0.6 0.8 broadcast_in_dim.8
  1.5 24.4 %all_to_all.35 = bf16[32,8,576]{2,1,0:T(8,128)(2,1)S(1)} all-to-all(bf16[32,8,576]{2,1,0:T(8,128)(2,1)S(1)} %broadcast_in_dim.8), channel_id=1, replica_groups=mesh['zh'=4,'zm'=2,'zb'=2,'xh'=2,'y'=4,'xl'=2,'core'=2] {'zb','xh','y','..., dimensions={0} | all-to-all | bytes 589824 | tf_op jit(solution)/shard_map/all_to_all | solution.py:20
  25.9 1.1 convolution_convert_fusion.1
  26.9 5.8 %all-to-all-start.1 = ((bf16[4,64,512]{2,1,0:T(8,128)(2,1)}), bf16[4,64,512]{2,1,0:T(8,128)(2,1)S(1)}, u32[]{:S(2)}, u32[]{:S(2)}) async-start(bf16[4,64,512]{2,1,0:T(8,128)(2,1)} %bitcast.3), calls=%async_computation.1 | async-start | bytes 524288 | tf_op jit(solution)/shard_map/all_to_all | solution.py:20
  33.4 4.5 %all-to-all-done.1 = bf16[4,64,512]{2,1,0:T(8,128)(2,1)S(1)} async-done(((bf16[4,64,512]{2,1,0:T(8,128)(2,1)}), bf16[4,64,512]{2,1,0:T(8,128)(2,1)S(1)}, u32[]{:S(2)}, u32[]{:S(2)}) %all-to-all-start.1) | async-done | bytes 262176 | tf_op jit(solution)/shard_map/all_to_all | solution.py:20
  37.9 0.2 multiply_convert_fusion
  38.2 9.8 %collective-permute-start = (bf16[64,256]{1,0:T(8,128)(2,1)S(1)}, bf16[64,256]{1,0:T(8,128)(2,1)S(1)}, u32[]{:S(2)}, u32[]{:S(2)}) collective-permute-start(bf16[64,256]{1,0:T(8,128)(2,1)S(1)} %get-tuple-element.7), channel_id=1, source_target_pairs={{0,384},{128,256},{256,128},{384,0},{1,385},{129,257},{257,129},{3... | collective-permute-start | bytes 98312 | tf_op jit(solution)/shard_map/ppermute | solution.py:29
  47.9 1.5 collective-permute-done
  49.4 7.3 %all_gather.6.codes_ref = bf16[256,512]{1,0:T(8,128)(2,1)S(1)} all-gather(bf16[64,512]{1,0:T(8,128)(2,1)S(1)} %pad_maximum_fusion), channel_id=1, replica_groups=mesh['zh'=4,'zm'=2,'zb'=2,'xh'=2,'y'=4,'xl'=2,'core'=2] {'xl','core'}, dimensions={0}, use_global_device_ids=true | all-gather | bytes 327680 | tf_op jit(solution)/shard_map/all_gather | solution.py:124
  56.7 1.0 shard_map.102
  57.7 24.1 %all_to_all.36 = bf16[16,4,16,576]{3,2,1,0:T(8,128)(2,1)} all-to-all(bf16[16,4,16,576]{3,2,1,0:T(8,128)(2,1)S(1)} %shard_map.102), channel_id=1, replica_groups=mesh['zh'=4,'zm'=2,'zb'=2,'xh'=2,'y'=4,'xl'=2,'core'=2] {'zb','xh','y'}, dimensions={0} | all-to-all | bytes 2359296 | tf_op jit(solution)/shard_map/all_to_all | solution.py:20
  81.8 1.5 reduce_sum.49
  83.3 21.9 %all_to_all.37 = bf16[8,8,576]{2,1,0:T(8,128)(2,1)S(1)} all-to-all(bf16[8,8,576]{2,1,0:T(8,128)(2,1)S(1)} %bitcast.19), channel_id=1, replica_groups=mesh['zh'=4,'zm'=2,'zb'=2,'xh'=2,'y'=4,'xl'=2,'core'=2] {'zh','zm'}, dimensions={0} | all-to-all | bytes 147456 | tf_op jit(solution)/shard_map/all_to_all | solution.py:20
  105.2 0.6 subtract_convert_fusion
  105.8 14.9 %all_to_all.38 = bf16[8,8,576]{2,1,0:T(8,128)(2,1)S(1)} all-to-all(bf16[8,8,576]{2,1,0:T(8,128)(2,1)S(1)} %broadcast_in_dim.9), channel_id=1, replica_groups=mesh['zh'=4,'zm'=2,'zb'=2,'xh'=2,'y'=4,'xl'=2,'core'=2] {'zh','zm'}, dimensions={0} | all-to-all | bytes 147456 | tf_op jit(solution)/shard_map/all_to_all | solution.py:20
  120.9 18.8 %all_to_all.39.error_ref = bf16[16,4,16,576]{3,2,1,0:T(8,128)(2,1)S(1)} all-to-all(bf16[16,4,16,576]{3,2,1,0:T(8,128)(2,1)S(1)} %broadcast_in_dim.11), channel_id=1, replica_groups=mesh['zh'=4,'zm'=2,'zb'=2,'xh'=2,'y'=4,'xl'=2,'core'=2] {'zb','xh','y'}, dimensions={0} | all-to-all | bytes 2359296 | tf_op jit(solution)/shard_map/all_to_all | solution.py:20
  139.7 1.0 shard_map.103
  140.7 13.2 %all_to_all.40 = bf16[4,64,512]{2,1,0:T(8,128)(2,1)S(1)} all-to-all(bf16[4,64,512]{2,1,0:T(8,128)(2,1)S(1)} %bitcast.17), channel_id=1, replica_groups=mesh['zh'=4,'zm'=2,'zb'=2,'xh'=2,'y'=4,'xl'=2,'core'=2] {'xl','core'}, dimensions={0} | all-to-all | bytes 524288 | tf_op jit(solution)/shard_map/all_to_all | solution.py:20
  154.0 2.0 %collective-permute-start.1 = (bf16[64,256]{1,0:T(8,128)(2,1)S(1)}, bf16[64,256]{1,0:T(8,128)(2,1)S(1)}, u32[]{:S(2)}, u32[]{:S(2)}) collective-permute-start(bf16[64,256]{1,0:T(8,128)(2,1)S(1)} %slice.28), channel_id=1, source_target_pairs={{0,384},{128,256},{256,128},{384,0},{1,385},{129,257},{257,129},{3... | collective-permute-start | bytes 98312 | tf_op jit(solution)/shard_map/ppermute | solution.py:29
  156.0 1.8 %shard_map.104 = bf16[576,1280]{1,0:T(8,128)(2,1)} custom-call(s32[1]{0:T(128)} %bitcast.source_ref, bf16[16,4,16,576]{3,2,1,0:T(8,128)(2,1)S(1)} %all_to_all.39.error_ref, bf16[256,512]{1,0:T(8,128)(2,1)S(1)} %all_gather.6.codes_ref), custom_call_target="tpu_custom_call" | custom-call | flops 377487360 | bytes 3000000 | tf_op jit(solution)/shard_map/pallas_call | solution.py:89
  157.8 4.8 %collective-permute-done.1 = bf16[64,256]{1,0:T(8,128)(2,1)S(1)} collective-permute-done((bf16[64,256]{1,0:T(8,128)(2,1)S(1)}, bf16[64,256]{1,0:T(8,128)(2,1)S(1)}, u32[]{:S(2)}, u32[]{:S(2)}) %collective-permute-start.1) | collective-permute-done | bytes 32800 | tf_op jit(solution)/shard_map/ppermute | solution.py:29
  162.6 7.8 %all_gather.7 = bf16[256,512]{1,0:T(8,128)(2,1)S(1)} all-gather(bf16[64,512]{1,0:T(8,128)(2,1)S(1)} %fusion.4), channel_id=1, replica_groups=mesh['zh'=4,'zm'=2,'zb'=2,'xh'=2,'y'=4,'xl'=2,'core'=2] {'xl','core'}, dimensions={0}, use_global_device_ids=true | all-gather | bytes 327680 | tf_op jit(solution)/shard_map/all_gather | solution.py:148
  170.4 0.6 convert_reduce_fusion
  171.0 1.2 convolution_convert_fusion
  (21 shorter events, 0.3 us)
Async XLA Ops:
  0.6 25.2 %copy-start = (bf16[512,576]{0,1:T(8,128)(2,1)S(1)}, bf16[512,576]{0,1:T(8,128)(2,1)}, u32[]{:S(2)}) copy-start(bf16[512,576]{0,1:T(8,128)(2,1)} %param.9) | copy-start | bytes 1769476
  1.4 36.5 %copy-start.2 = (s32[512,256]{1,0:T(8,128)S(1)}, s32[512,256]{1,0:T(8,128)}, u32[]{:S(2)}) copy-start(s32[512,256]{1,0:T(8,128)} %param.11) | copy-start | bytes 1572868
  1.4 36.5 %copy-start.4 = (f32[512]{0:T(512)S(1)}, f32[512]{0:T(512)}, u32[]{:S(2)}) copy-start(f32[512]{0:T(512)} %param.10) | copy-start | bytes 6148
  26.9 29.7 %copy-start.1 = (bf16[1280,576]{0,1:T(8,128)(2,1)S(1)}, bf16[1280,576]{0,1:T(8,128)(2,1)}, u32[]{:S(2)}) copy-start(bf16[1280,576]{0,1:T(8,128)(2,1)} %param.12) | copy-start | bytes 4423684
  26.9 10.9 %all-to-all-start.1 = ((bf16[4,64,512]{2,1,0:T(8,128)(2,1)}), bf16[4,64,512]{2,1,0:T(8,128)(2,1)S(1)}, u32[]{:S(2)}, u32[]{:S(2)}) async-start(bf16[4,64,512]{2,1,0:T(8,128)(2,1)} %bitcast.3), calls=%async_computation.1 | async-start | bytes 524288 | tf_op jit(solution)/shard_map/all_to_all | solution.py:20
  38.2 11.3 %collective-permute-start = (bf16[64,256]{1,0:T(8,128)(2,1)S(1)}, bf16[64,256]{1,0:T(8,128)(2,1)S(1)}, u32[]{:S(2)}, u32[]{:S(2)}) collective-permute-start(bf16[64,256]{1,0:T(8,128)(2,1)S(1)} %get-tuple-element.7), channel_id=1, source_target_pairs={{0,384},{128,256},{256,128},{384,0},{1,385},{129,257},{257,129},{3... | collective-permute-start | bytes 98312 | tf_op jit(solution)/shard_map/ppermute | solution.py:29
  81.8 23.4 %copy-start.3 = (bf16[8,576]{1,0:T(8,128)(2,1)S(1)}, bf16[8,576]{1,0:T(8,128)(2,1)}, u32[]{:S(2)}) copy-start(bf16[8,576]{1,0:T(8,128)(2,1)} %param.8) | copy-start | bytes 27652
  154.0 8.6 %collective-permute-start.1 = (bf16[64,256]{1,0:T(8,128)(2,1)S(1)}, bf16[64,256]{1,0:T(8,128)(2,1)S(1)}, u32[]{:S(2)}, u32[]{:S(2)}) collective-permute-start(bf16[64,256]{1,0:T(8,128)(2,1)S(1)} %slice.28), channel_id=1, source_target_pairs={{0,384},{128,256},{256,128},{384,0},{1,385},{129,257},{257,129},{3... | collective-permute-start | bytes 98312 | tf_op jit(solution)/shard_map/ppermute | solution.py:29

commit v3 on v2

--- a/solution.py
+++ b/solution.py
@@ -13,7 +13,7 @@
 FAR = ("zh", "zm")
 FEAT = ("xl", "core")
 BLK = ("zh", "zm", "zb", "xh", "y")
-VMEM_BYTES = 40 * 1024 * 1024
+VMEM_BYTES = 16 * 1024 * 1024
 
 
 def exchange(pieces, axes):
@@ -27,6 +27,10 @@
 
 def mirror(piece):
     return lax.ppermute(piece, "zh", [(s, LAYERS - 1 - s) for s in range(LAYERS)])
+
+
+def array(shape, dtype=BF):
+    return jax.ShapeDtypeStruct(shape, dtype)
 
 
 def own_slot(source, target):
@@ -83,14 +87,33 @@
         out_ref[:, slot * span : (slot + 1) * span] = grad.astype(BF)
 
 
-def call(kernel, shape, flops, moved, *operands):
-    specs = [pl.BlockSpec(memory_space=pltpu.SMEM)]
-    specs += [pl.BlockSpec(memory_space=pltpu.VMEM)] * (len(operands) - 1)
+def pre_kernel(inputs_ref, weight_ref, out_ref):
+    pre = jnp.dot(inputs_ref[...], weight_ref[...], preferred_element_type=F32)
+    out_ref[...] = pre.astype(BF)
+
+
+def sum_kernel(pieces_ref, out_ref):
+    for target in range(LAYERS):
+        out_ref[target] = jnp.sum(pieces_ref[:, target].astype(F32), axis=0).astype(BF)
+
+
+def enc_grad_kernel(inputs_ref, grad_ref, out_ref, bias_ref):
+    grad = grad_ref[...]
+    total = lax.dot_general(
+        inputs_ref[...], grad, (((0,), (0,)), ((), ())), preferred_element_type=F32
+    )
+    out_ref[...] = total.astype(BF)
+    bias_ref[...] = jnp.sum(grad.astype(F32), axis=0, keepdims=True)
+
+
+def call(kernel, shapes, flops, moved, *operands):
+    where = [pltpu.SMEM if operand.dtype == jnp.int32 else pltpu.VMEM for operand in operands]
+    outs = jax.tree.map(lambda _: pl.BlockSpec(memory_space=pltpu.VMEM), shapes)
     return pl.pallas_call(
         kernel,
-        out_shape=jax.ShapeDtypeStruct(shape, BF),
-        in_specs=specs,
-        out_specs=pl.BlockSpec(memory_space=pltpu.VMEM),
+        out_shape=shapes,
+        in_specs=[pl.BlockSpec(memory_space=space) for space in where],
+        out_specs=outs,
         compiler_params=pltpu.CompilerParams(vmem_limit_bytes=VMEM_BYTES),
         cost_estimate=pl.CostEstimate(flops=flops, bytes_accessed=moved, transcendentals=0),
     )(*operands)
@@ -114,8 +137,10 @@
     dec = dec_weight.T
 
     own_inputs = share(layer_inputs, NEAR + ("zm",)).reshape(tokens, width)
-    pre_part = jnp.einsum("md,fd->mf", own_inputs, enc_weight, preferred_element_type=F32)
-    pre_part = pre_part.astype(BF).reshape(parts, quarter, feats)
+    pre_part = call(
+        pre_kernel, array((tokens, feats)), 2 * tokens * feats * width, 1200000,
+        own_inputs, enc_weight.T,
+    ).reshape(parts, quarter, feats)
     pre = jnp.sum(exchange(pre_part, FEAT).astype(F32), axis=0) + enc_bias[None, :]
     code_q = (mask_q * pre).astype(BF)
     low, high = code_q[:, :span], code_q[:, span:]
@@ -124,35 +149,40 @@
     codes = lax.all_gather(both_q, FEAT, axis=0, tiled=True)
 
     pieces = call(
-        recon_kernel, (near, LAYERS, zm * rows, width), 8 * 2 * tokens * span * width, 3000000,
+        recon_kernel, array((near, LAYERS, zm * rows, width)), 8 * 2 * tokens * span * width, 3000000,
         source, codes, dec,
     )
-    sums = jnp.sum(exchange(pieces, NEAR).astype(F32), axis=0).astype(BF)
-    sums = sums.reshape(far, rows, width)
+    sums = call(
+        sum_kernel, array((LAYERS, zm * rows, width)), tokens * LAYERS * width, 1300000,
+        exchange(pieces, NEAR),
+    ).reshape(far, rows, width)
     recon_rows = jnp.sum(exchange(sums, FAR).astype(F32), axis=0)
     error_rows = (recon_rows - mlp_targets.astype(F32)).astype(BF)
     error = share(error_rows, FAR).reshape(LAYERS, zm * rows, width)
     error = share(error, NEAR).reshape(near, LAYERS, zm * rows, width)
 
     terms = call(
-        terms_kernel, (tokens, feats), 8 * 2 * tokens * span * width, 3000000,
+        terms_kernel, array((tokens, feats)), 8 * 2 * tokens * span * width, 3000000,
         source, error, dec,
     )
     terms = exchange(terms.reshape(parts, quarter, feats), FEAT)
     terms_q = jnp.sum(terms.astype(F32), axis=0)
+    terms_q, recon_rows = lax.optimization_barrier((terms_q, recon_rows))
     returned = mirror(terms_q[:, span:].astype(BF)).astype(F32)
     own = terms_q[:, :span]
     grad_q = jnp.concatenate(
         [jnp.where(first, own, returned), jnp.where(first, returned, own)], axis=1
     )
     pre_grad = lax.all_gather((mask_q * grad_q).astype(BF), FEAT, axis=0, tiled=True)
-    bias_grad = jnp.sum(pre_grad.astype(F32), axis=0)
-    enc_grad = jnp.einsum("mf,md->fd", pre_grad, own_inputs, preferred_element_type=F32)
+    enc_grad, bias_grad = call(
+        enc_grad_kernel, (array((width, feats)), array((1, feats), F32)),
+        2 * tokens * feats * width, 1200000, own_inputs, pre_grad,
+    )
     dec_grad = call(
-        dec_grad_kernel, dec.shape, 5 * 2 * tokens * span * width, 3000000,
+        dec_grad_kernel, array(dec.shape), 5 * 2 * tokens * span * width, 3000000,
         source, error, codes,
     )
-    return (recon_rows.astype(BF), enc_grad.astype(BF), bias_grad, dec_grad.T)
+    return (recon_rows.astype(BF), enc_grad.T, bias_grad[0], dec_grad.T)
 
 
 def solution(mesh):

time: 173 us -> 169 us (0.977)
  Pallas kernels: 3.77 us -> 6.2 us
  matrix products: 2.46 us -> 0.21 us
  other arithmetic: 2.92 us -> 0.77 us
    pallas_call x3 -> x6, Pallas kernels: 3.77 us -> 6.2 us  [call(): pl.pallas_call(kernel, out_shape=shapes, in_specs=[pl.BlockSpec(memory_sp...]
    dot_general x2 -> x0, matrix products: 2.25 us -> none  [the longest x1 1.17 us: body(): jnp.einsum('mf,md->fd', pre_grad, own_inputs, preferred_element_type=F32)]
    reduce_sum x2 -> x0, other arithmetic: 2.16 us -> none  [the longest x1 1.53 us: body(): sums = jnp.sum(exchange(pieces, NEAR).astype(F32), axis=0).astype(BF)]
where the time goes in v3:
time: 169 us
  blocking collectives  132 us (78%)
  starting transfers between devices  17.6 us (10%)
  waiting for transfers between devices  10.1 us (6%)
  Pallas kernels  6.2 us (4%)
    all_to_all x6, blocking collectives, exchange(): return lax.all_to_all(pieces, axes, 0, 0, tiled=True)  117 us
    ppermute x2, starting transfers between devices, mirror(): lax.ppermute(piece, 'zh', [(s, LAYERS - 1 - s) for s in range(LAYERS)])  11.8 us
    all_gather x1, blocking collectives, body(): lax.all_gather((mask_q * grad_q).astype(BF), FEAT, axis=0, tiled=True)  7.81 us
    all_gather x1, blocking collectives, body(): codes = lax.all_gather(both_q, FEAT, axis=0, tiled=True)  7.25 us
    pallas_call x6, Pallas kernels, call(): pl.pallas_call(kernel, out_shape=shapes, in_specs=[pl.BlockSpec(memory_sp...  6.2 us
    all_to_all x1, starting transfers between devices, exchange(): return lax.all_to_all(pieces, axes, 0, 0, tiled=True)  5.77 us
    ppermute x2, waiting for transfers between devices, mirror(): lax.ppermute(piece, 'zh', [(s, LAYERS - 1 - s) for s in range(LAYERS)])  5.6 us
    all_to_all x1, waiting for transfers between devices, exchange(): return lax.all_to_all(pieces, axes, 0, 0, tiled=True)  4.49 us
  transfers between devices with their start and end apart: 3, of which 3 were waited for; matrix products, arithmetic and copies ran while one was open for 0% of the time, Pallas kernels for 1%

profile of v3, /device:TPU:1, one launch (start us, length us, event | category | flops | bytes accessed | tf_op | source)
XLA Modules:
  0.0 168.9 jit_solution(6896011845203729118)
XLA Ops:
  0.6 0.8 broadcast_in_dim.8
  1.5 24.4 %all_to_all.35 = bf16[32,8,576]{2,1,0:T(8,128)(2,1)S(1)} all-to-all(bf16[32,8,576]{2,1,0:T(8,128)(2,1)S(1)} %broadcast_in_dim.8), channel_id=1, replica_groups=mesh['zh'=4,'zm'=2,'zb'=2,'xh'=2,'y'=4,'xl'=2,'core'=2] {'zb','xh','y','..., dimensions={0} | all-to-all | bytes 589824 | tf_op jit(solution)/shard_map/all_to_all | solution.py:20
  25.9 1.1 shard_map.102
  26.9 5.8 %all-to-all-start.1 = ((bf16[4,64,512]{2,1,0:T(8,128)(2,1)}), bf16[4,64,512]{2,1,0:T(8,128)(2,1)S(1)}, u32[]{:S(2)}, u32[]{:S(2)}) async-start(bf16[4,64,512]{2,1,0:T(8,128)(2,1)} %bitcast.4), calls=%async_computation.1 | async-start | bytes 524288 | tf_op jit(solution)/shard_map/all_to_all | solution.py:20
  33.4 4.5 %all-to-all-done.1 = bf16[4,64,512]{2,1,0:T(8,128)(2,1)S(1)} async-done(((bf16[4,64,512]{2,1,0:T(8,128)(2,1)}), bf16[4,64,512]{2,1,0:T(8,128)(2,1)S(1)}, u32[]{:S(2)}, u32[]{:S(2)}) %all-to-all-start.1) | async-done | bytes 262176 | tf_op jit(solution)/shard_map/all_to_all | solution.py:20
  37.9 0.2 multiply_convert_fusion
  38.2 9.8 %collective-permute-start = (bf16[64,256]{1,0:T(8,128)(2,1)S(1)}, bf16[64,256]{1,0:T(8,128)(2,1)S(1)}, u32[]{:S(2)}, u32[]{:S(2)}) collective-permute-start(bf16[64,256]{1,0:T(8,128)(2,1)S(1)} %get-tuple-element.15), channel_id=1, source_target_pairs={{0,384},{128,256},{256,128},{384,0},{1,385},{129,257},{257,129},{3... | collective-permute-start | bytes 98312 | tf_op jit(solution)/shard_map/ppermute | solution.py:29
  47.9 1.5 collective-permute-done
  49.4 7.2 %all_gather.6.codes_ref = bf16[256,512]{1,0:T(8,128)(2,1)S(1)} all-gather(bf16[64,512]{1,0:T(8,128)(2,1)S(1)} %pad_maximum_fusion), channel_id=1, replica_groups=mesh['zh'=4,'zm'=2,'zb'=2,'xh'=2,'y'=4,'xl'=2,'core'=2] {'xl','core'}, dimensions={0}, use_global_device_ids=true | all-gather | bytes 327680 | tf_op jit(solution)/shard_map/all_gather | solution.py:149
  56.7 1.0 shard_map.103
  57.7 23.4 %all_to_all.36.pieces_ref = bf16[16,4,16,576]{3,2,1,0:T(8,128)(2,1)S(1)} all-to-all(bf16[16,4,16,576]{3,2,1,0:T(8,128)(2,1)S(1)} %shard_map.103), channel_id=1, replica_groups=mesh['zh'=4,'zm'=2,'zb'=2,'xh'=2,'y'=4,'xl'=2,'core'=2] {'zb','xh','y'}, dimensions={0} | all-to-all | bytes 2359296 | tf_op jit(solution)/shard_map/all_to_all | solution.py:20
  81.1 0.2 shard_map.104
  81.3 22.1 %all_to_all.37 = bf16[8,8,576]{2,1,0:T(8,128)(2,1)S(1)} all-to-all(bf16[8,8,576]{2,1,0:T(8,128)(2,1)S(1)} %bitcast.18), channel_id=1, replica_groups=mesh['zh'=4,'zm'=2,'zb'=2,'xh'=2,'y'=4,'xl'=2,'core'=2] {'zh','zm'}, dimensions={0} | all-to-all | bytes 147456 | tf_op jit(solution)/shard_map/all_to_all | solution.py:20
  103.4 14.7 %all_to_all.38 = bf16[8,8,576]{2,1,0:T(8,128)(2,1)S(1)} all-to-all(bf16[8,8,576]{2,1,0:T(8,128)(2,1)S(1)} %broadcast_in_dim.9), channel_id=1, replica_groups=mesh['zh'=4,'zm'=2,'zb'=2,'xh'=2,'y'=4,'xl'=2,'core'=2] {'zh','zm'}, dimensions={0} | all-to-all | bytes 147456 | tf_op jit(solution)/shard_map/all_to_all | solution.py:20
  118.1 0.2 broadcast_in_dim.11
  118.3 18.7 %all_to_all.39.error_ref = bf16[16,4,16,576]{3,2,1,0:T(8,128)(2,1)S(1)} all-to-all(bf16[16,4,16,576]{3,2,1,0:T(8,128)(2,1)S(1)} %broadcast_in_dim.11), channel_id=1, replica_groups=mesh['zh'=4,'zm'=2,'zb'=2,'xh'=2,'y'=4,'xl'=2,'core'=2] {'zb','xh','y'}, dimensions={0} | all-to-all | bytes 2359296 | tf_op jit(solution)/shard_map/all_to_all | solution.py:20
  137.0 1.0 shard_map.105
  138.0 13.3 %all_to_all.40 = bf16[4,64,512]{2,1,0:T(8,128)(2,1)S(1)} all-to-all(bf16[4,64,512]{2,1,0:T(8,128)(2,1)S(1)} %bitcast.16), channel_id=1, replica_groups=mesh['zh'=4,'zm'=2,'zb'=2,'xh'=2,'y'=4,'xl'=2,'core'=2] {'xl','core'}, dimensions={0} | all-to-all | bytes 524288 | tf_op jit(solution)/shard_map/all_to_all | solution.py:20
  151.4 2.1 %collective-permute-start.1 = (bf16[64,256]{1,0:T(8,128)(2,1)S(1)}, bf16[64,256]{1,0:T(8,128)(2,1)S(1)}, u32[]{:S(2)}, u32[]{:S(2)}) collective-permute-start(bf16[64,256]{1,0:T(8,128)(2,1)S(1)} %slice.27), channel_id=1, source_target_pairs={{0,384},{128,256},{256,128},{384,0},{1,385},{129,257},{257,129},{3... | collective-permute-start | bytes 98312 | tf_op jit(solution)/shard_map/ppermute | solution.py:29
  153.5 1.8 %shard_map.107 = bf16[576,1280]{1,0:T(8,128)(2,1)} custom-call(s32[1]{0:T(128)} %bitcast.source_ref, bf16[16,4,16,576]{3,2,1,0:T(8,128)(2,1)S(1)} %all_to_all.39.error_ref, bf16[256,512]{1,0:T(8,128)(2,1)S(1)} %all_gather.6.codes_ref), custom_call_target="tpu_custom_call" | custom-call | flops 377487360 | bytes 3000000 | tf_op jit(solution)/shard_map/pallas_call | solution.py:112
  155.2 0.6 convert_element_type.39
  155.8 4.1 %collective-permute-done.1 = bf16[64,256]{1,0:T(8,128)(2,1)S(1)} collective-permute-done((bf16[64,256]{1,0:T(8,128)(2,1)S(1)}, bf16[64,256]{1,0:T(8,128)(2,1)S(1)}, u32[]{:S(2)}, u32[]{:S(2)}) %collective-permute-start.1) | collective-permute-done | bytes 32800 | tf_op jit(solution)/shard_map/ppermute | solution.py:29
  160.0 7.8 %all_gather.7.grad_ref = bf16[256,512]{1,0:T(8,128)(2,1)S(1)} all-gather(bf16[64,512]{1,0:T(8,128)(2,1)S(1)} %fusion.2), channel_id=1, replica_groups=mesh['zh'=4,'zm'=2,'zb'=2,'xh'=2,'y'=4,'xl'=2,'core'=2] {'xl','core'}, dimensions={0}, use_global_device_ids=true | all-gather | bytes 327680 | tf_op jit(solution)/shard_map/all_gather | solution.py:176
  167.8 1.2 shard_map.106
  (21 shorter events, 0.2 us)
Async XLA Ops:
  0.6 25.2 %copy-start.1 = (bf16[512,576]{0,1:T(8,128)(2,1)S(1)}, bf16[512,576]{0,1:T(8,128)(2,1)}, u32[]{:S(2)}) copy-start(bf16[512,576]{0,1:T(8,128)(2,1)} %param.9) | copy-start | bytes 1769476
  1.4 36.5 %copy-start.2 = (s32[512,256]{1,0:T(8,128)S(1)}, s32[512,256]{1,0:T(8,128)}, u32[]{:S(2)}) copy-start(s32[512,256]{1,0:T(8,128)} %param.11) | copy-start | bytes 1572868
  1.4 36.5 %copy-start.4 = (f32[512]{0:T(512)S(1)}, f32[512]{0:T(512)}, u32[]{:S(2)}) copy-start(f32[512]{0:T(512)} %param.10) | copy-start | bytes 6148
  26.9 29.7 %copy-start = (bf16[1280,576]{0,1:T(8,128)(2,1)S(1)}, bf16[1280,576]{0,1:T(8,128)(2,1)}, u32[]{:S(2)}) copy-start(bf16[1280,576]{0,1:T(8,128)(2,1)} %param.12) | copy-start | bytes 4423684
  26.9 10.9 %all-to-all-start.1 = ((bf16[4,64,512]{2,1,0:T(8,128)(2,1)}), bf16[4,64,512]{2,1,0:T(8,128)(2,1)S(1)}, u32[]{:S(2)}, u32[]{:S(2)}) async-start(bf16[4,64,512]{2,1,0:T(8,128)(2,1)} %bitcast.4), calls=%async_computation.1 | async-start | bytes 524288 | tf_op jit(solution)/shard_map/all_to_all | solution.py:20
  38.2 11.3 %collective-permute-start = (bf16[64,256]{1,0:T(8,128)(2,1)S(1)}, bf16[64,256]{1,0:T(8,128)(2,1)S(1)}, u32[]{:S(2)}, u32[]{:S(2)}) collective-permute-start(bf16[64,256]{1,0:T(8,128)(2,1)S(1)} %get-tuple-element.15), channel_id=1, source_target_pairs={{0,384},{128,256},{256,128},{384,0},{1,385},{129,257},{257,129},{3... | collective-permute-start | bytes 98312 | tf_op jit(solution)/shard_map/ppermute | solution.py:29
  81.1 22.3 %copy-start.3 = (bf16[8,576]{1,0:T(8,128)(2,1)S(1)}, bf16[8,576]{1,0:T(8,128)(2,1)}, u32[]{:S(2)}) copy-start(bf16[8,576]{1,0:T(8,128)(2,1)} %param.8) | copy-start | bytes 27652
  151.4 8.6 %collective-permute-start.1 = (bf16[64,256]{1,0:T(8,128)(2,1)S(1)}, bf16[64,256]{1,0:T(8,128)(2,1)S(1)}, u32[]{:S(2)}, u32[]{:S(2)}) collective-permute-start(bf16[64,256]{1,0:T(8,128)(2,1)S(1)} %slice.27), channel_id=1, source_target_pairs={{0,384},{128,256},{256,128},{384,0},{1,385},{129,257},{257,129},{3... | collective-permute-start | bytes 98312 | tf_op jit(solution)/shard_map/ppermute | solution.py:29

commit v4 on v3

--- a/solution.py
+++ b/solution.py
@@ -10,7 +10,6 @@
 F32 = jnp.float32
 AXES = ("zh", "zm", "zb", "xh", "y", "xl", "core")
 NEAR = ("zb", "xh", "y")
-FAR = ("zh", "zm")
 FEAT = ("xl", "core")
 BLK = ("zh", "zm", "zb", "xh", "y")
 VMEM_BYTES = 16 * 1024 * 1024
@@ -25,8 +24,22 @@
     return exchange(jnp.broadcast_to(piece[None], (count,) + piece.shape), axes)
 
 
+MIRRORED = [[0, 3], [1, 2]]
+ADJACENT = [[0, 1], [2, 3]]
+
+
 def mirror(piece):
     return lax.ppermute(piece, "zh", [(s, LAYERS - 1 - s) for s in range(LAYERS)])
+
+
+def both_of(piece, pairs):
+    layer = lax.axis_index("zh")
+    second = sum((layer == pair[1]).astype(jnp.int32) for pair in pairs)
+    return lax.all_gather(piece, "zh", axis=0, axis_index_groups=pairs), 1 - second
+
+
+def pick(pair, place):
+    return jnp.where(place == 0, pair[0], pair[1])
 
 
 def array(shape, dtype=BF):
@@ -94,7 +107,7 @@
 
 def sum_kernel(pieces_ref, out_ref):
     for target in range(LAYERS):
-        out_ref[target] = jnp.sum(pieces_ref[:, target].astype(F32), axis=0).astype(BF)
+        out_ref[target] = jnp.sum(pieces_ref[:, target].astype(F32), axis=0)
 
 
 def enc_grad_kernel(inputs_ref, grad_ref, out_ref, bias_ref):
@@ -126,7 +139,7 @@
     feats, tokens = act_mask.shape
     span = feats // 2
     parts = lax.axis_size(FEAT)
-    near, far = lax.axis_size(NEAR), lax.axis_size(FAR)
+    near = lax.axis_size(NEAR)
     zm = lax.axis_size("zm")
     quarter = tokens // parts
 
@@ -144,7 +157,7 @@
     pre = jnp.sum(exchange(pre_part, FEAT).astype(F32), axis=0) + enc_bias[None, :]
     code_q = (mask_q * pre).astype(BF)
     low, high = code_q[:, :span], code_q[:, span:]
-    received = mirror(jnp.where(first, high, low))
+    received = pick(*both_of(jnp.where(first, high, low), MIRRORED))
     both_q = jnp.concatenate([jnp.where(first, low, high), received], axis=1)
     codes = lax.all_gather(both_q, FEAT, axis=0, tiled=True)
 
@@ -152,13 +165,28 @@
         recon_kernel, array((near, LAYERS, zm * rows, width)), 8 * 2 * tokens * span * width, 3000000,
         source, codes, dec,
     )
+    block = (LAYERS, zm, rows, width)
     sums = call(
-        sum_kernel, array((LAYERS, zm * rows, width)), tokens * LAYERS * width, 1300000,
+        sum_kernel, array((LAYERS, zm * rows, width), F32), tokens * LAYERS * width, 1400000,
         exchange(pieces, NEAR),
-    ).reshape(far, rows, width)
-    recon_rows = jnp.sum(exchange(sums, FAR).astype(F32), axis=0)
-    error_rows = (recon_rows - mlp_targets.astype(F32)).astype(BF)
-    error = share(error_rows, FAR).reshape(LAYERS, zm * rows, width)
+    ).reshape(block)
+    sums, targets = lax.optimization_barrier((sums, mlp_targets))
+    layer, place = lax.axis_index("zh"), lax.axis_index("zm")
+    mine = jnp.arange(LAYERS)[:, None] == layer
+    mine = (mine & (jnp.arange(zm)[None, :] == place))[:, :, None, None]
+    part = (sums - jnp.where(mine, targets.astype(F32)[None, None], 0.0)).astype(BF)
+
+    def own_rows(array):
+        return lax.dynamic_slice(array, (layer, place, 0, 0), (1, 1, rows, width))[0, 0]
+
+    near_pair = lax.all_gather(part.reshape(LAYERS, zm * rows, width), "zm", axis=0)
+    arrived = [(near_pair, 1 - place)]
+    part = jnp.sum(near_pair.astype(F32), axis=0).astype(BF)
+    for pairs in (MIRRORED, ADJACENT):
+        pair, other = both_of(part, pairs)
+        arrived.append((pair, other))
+        part = jnp.sum(pair.astype(F32), axis=0).astype(BF)
+    error = part
     error = share(error, NEAR).reshape(near, LAYERS, zm * rows, width)
 
     terms = call(
@@ -167,7 +195,10 @@
     )
     terms = exchange(terms.reshape(parts, quarter, feats), FEAT)
     terms_q = jnp.sum(terms.astype(F32), axis=0)
-    terms_q, recon_rows = lax.optimization_barrier((terms_q, recon_rows))
+    terms_q, sums, arrived = lax.optimization_barrier((terms_q, sums, arrived))
+    recon_rows = own_rows(sums)
+    for pair, other in arrived:
+        recon_rows += own_rows(pick(pair, other).reshape(block)).astype(F32)
     returned = mirror(terms_q[:, span:].astype(BF)).astype(F32)
     own = terms_q[:, :span]
     grad_q = jnp.concatenate(

time: 169 us -> 164 us (0.970)
  blocking collectives: 132 us -> 96.4 us
  waiting for transfers between devices: 10.1 us -> 30.5 us
  starting transfers between devices: 17.6 us -> 23.8 us
  local copies, waits for them, and re-layouts: 0.98 us -> 3.35 us
    all_to_all x6 -> x2, blocking collectives: 117 us -> 44.7 us  [exchange(): return lax.all_to_all(pieces, axes, 0, 0, tiled=True)]
    all_gather x0 -> x4, blocking collectives: none -> 36.9 us  [the longest x3 29.9 us: both_of(): lax.all_gather(piece, 'zh', axis=0, axis_index_groups=pairs)]
    all_to_all x1 -> x3, waiting for transfers between devices: 4.49 us -> 28.9 us  [exchange(): return lax.all_to_all(pieces, axes, 0, 0, tiled=True)]
    all_to_all x1 -> x3, starting transfers between devices: 5.77 us -> 17.4 us  [exchange(): return lax.all_to_all(pieces, axes, 0, 0, tiled=True)]
    ppermute x2 -> x1, starting transfers between devices: 11.8 us -> 6.37 us  [mirror(): lax.ppermute(piece, 'zh', [(s, LAYERS - 1 - s) for s in range(LAYERS)])]
    ppermute x2 -> x1, waiting for transfers between devices: 5.6 us -> 1.58 us  [mirror(): lax.ppermute(piece, 'zh', [(s, LAYERS - 1 - s) for s in range(LAYERS)])]
    unnamed x10 -> x28, local copies, waits for them, and re-layouts: 0.02 us -> 2.4 us
  transfers between devices with their start and end apart: 3 -> 4, of which waited for: 3 -> 4; matrix products, arithmetic and copies ran while one was open for 0% -> 0% of each run, Pallas kernels for 1% -> 1%
where the time goes in v4:
time: 164 us
  blocking collectives  96.4 us (59%)
  waiting for transfers between devices  30.5 us (19%)
  starting transfers between devices  23.8 us (15%)
  Pallas kernels  6.19 us (4%)
  local copies, waits for them, and re-layouts  3.35 us (2%)
    all_to_all x2, blocking collectives, exchange(): return lax.all_to_all(pieces, axes, 0, 0, tiled=True)  44.7 us
    all_gather x3, blocking collectives, both_of(): lax.all_gather(piece, 'zh', axis=0, axis_index_groups=pairs)  29.9 us
    all_to_all x3, waiting for transfers between devices, exchange(): return lax.all_to_all(pieces, axes, 0, 0, tiled=True)  28.9 us
    all_to_all x3, starting transfers between devices, exchange(): return lax.all_to_all(pieces, axes, 0, 0, tiled=True)  17.4 us
    all_gather x1, blocking collectives, body(): lax.all_gather((mask_q * grad_q).astype(BF), FEAT, axis=0, tiled=True)  7.55 us
    all_gather x1, blocking collectives, body(): codes = lax.all_gather(both_q, FEAT, axis=0, tiled=True)  7.26 us
    all_gather x1, blocking collectives, body(): lax.all_gather(part.reshape(LAYERS, zm * rows, width), 'zm', axis=0)  7.03 us
    ppermute x1, starting transfers between devices, mirror(): lax.ppermute(piece, 'zh', [(s, LAYERS - 1 - s) for s in range(LAYERS)])  6.37 us
  transfers between devices with their start and end apart: 4, of which 4 were waited for; matrix products, arithmetic and copies ran while one was open for 0% of the time, Pallas kernels for 1%

profile of v4, /device:TPU:1, one launch (start us, length us, event | category | flops | bytes accessed | tf_op | source)
XLA Modules:
  0.0 163.8 jit_solution(8944502859573780665)
XLA Ops:
  0.6 0.8 broadcast_in_dim.17
  1.5 24.4 %all_to_all.25 = bf16[32,8,576]{2,1,0:T(8,128)(2,1)S(1)} all-to-all(bf16[32,8,576]{2,1,0:T(8,128)(2,1)S(1)} %broadcast_in_dim.17), channel_id=1, replica_groups=mesh['zh'=4,'zm'=2,'zb'=2,'xh'=2,'y'=4,'xl'=2,'core'=2] {'zb','xh','y','..., dimensions={0} | all-to-all | bytes 589824 | tf_op jit(solution)/shard_map/all_to_all | solution.py:19
  25.9 1.1 shard_map.102
  26.9 5.8 %all-to-all-start.1 = ((bf16[4,64,512]{2,1,0:T(8,128)(2,1)}), bf16[4,64,512]{2,1,0:T(8,128)(2,1)S(1)}, u32[]{:S(2)}, u32[]{:S(2)}) async-start(bf16[4,64,512]{2,1,0:T(8,128)(2,1)} %bitcast.4), calls=%async_computation.1 | async-start | bytes 524288 | tf_op jit(solution)/shard_map/all_to_all | solution.py:19
  33.4 4.5 %all-to-all-done.1 = bf16[4,64,512]{2,1,0:T(8,128)(2,1)S(1)} async-done(((bf16[4,64,512]{2,1,0:T(8,128)(2,1)}), bf16[4,64,512]{2,1,0:T(8,128)(2,1)S(1)}, u32[]{:S(2)}, u32[]{:S(2)}) %all-to-all-start.1) | async-done | bytes 262176 | tf_op jit(solution)/shard_map/all_to_all | solution.py:19
  37.9 0.9 multiply_convert_fusion
  38.8 10.0 %all-gather = bf16[128,256]{1,0:T(8,128)(2,1)S(1)} all-gather(bf16[64,256]{1,0:T(8,128)(2,1)S(1)} %get-tuple-element.31), channel_id=2, replica_groups={{0,384},{128,256},{1,385},{129,257},{2,386},{130,258},{3,387},{131,259}..., dimensions={0}, use_global_device_ids=true | all-gather | bytes 98304 | tf_op jit(solution)/shard_map/all_gather | solution.py:38
  48.8 7.3 %all_gather.29.codes_ref = bf16[256,512]{1,0:T(8,128)(2,1)S(1)} all-gather(bf16[64,512]{1,0:T(8,128)(2,1)S(1)} %pad_maximum_fusion), channel_id=1, replica_groups=mesh['zh'=4,'zm'=2,'zb'=2,'xh'=2,'y'=4,'xl'=2,'core'=2] {'xl','core'}, dimensions={0}, use_global_device_ids=true | all-gather | bytes 327680 | tf_op jit(solution)/shard_map/all_gather | solution.py:162
  56.1 1.0 shard_map.103
  57.1 1.0 copy-done.1
  58.2 3.7 %all-to-all-start.2 = ((bf16[16,4,16,576]{3,2,1,0:T(8,128)(2,1)}), bf16[16,4,16,576]{3,2,1,0:T(8,128)(2,1)S(1)}, u32[]{:S(2)}, u32[]{:S(2)}) async-start(bf16[16,4,16,576]{3,2,1,0:T(8,128)(2,1)} %copy-done.1), calls=%async_computation.2 | async-start | bytes 2621440 | tf_op jit(solution)/shard_map/all_to_all | solution.py:19
  62.0 21.0 %all-to-all-done.2.pieces_ref = bf16[16,4,16,576]{3,2,1,0:T(8,128)(2,1)S(1)} async-done(((bf16[16,4,16,576]{3,2,1,0:T(8,128)(2,1)}), bf16[16,4,16,576]{3,2,1,0:T(8,128)(2,1)S(1)}, u32[]{:S(2)}, u32[]{:S(2)}) %all-to-all-start.2) | async-done | bytes 1179680 | tf_op jit(solution)/shard_map/all_to_all | solution.py:19
  83.3 7.0 %all_gather.30 = bf16[2,4,16,576]{3,2,1,0:T(8,128)(2,1)S(1)} all-gather(bf16[1,4,16,576]{3,2,1,0:T(8,128)(2,1)S(1)} %fusion.3), channel_id=1, replica_groups=mesh['zh'=4,'zm'=2,'zb'=2,'xh'=2,'y'=4,'xl'=2,'core'=2] {'zm'}, dimensions={0}, use_global_device_ids=true | all-gather | bytes 221184 | tf_op jit(solution)/shard_map/all_gather | solution.py:182
  90.4 10.4 %all-gather.1 = bf16[8,16,576]{2,1,0:T(8,128)(2,1)S(1)} all-gather(bf16[4,16,576]{2,1,0:T(8,128)(2,1)S(1)} %reduce_sum.55), channel_id=3, replica_groups={{0,384},{128,256},{1,385},{129,257},{2,386},{130,258},{3,387},{131,259}..., dimensions={0}, use_global_device_ids=true | all-gather | bytes 221184 | tf_op jit(solution)/shard_map/all_gather | solution.py:38
  100.9 9.5 %all-gather.2 = bf16[8,16,576]{2,1,0:T(8,128)(2,1)S(1)} all-gather(bf16[4,16,576]{2,1,0:T(8,128)(2,1)S(1)} %reduce_sum.56), channel_id=4, replica_groups={{0,128},{256,384},{1,129},{257,385},{2,130},{258,386},{3,131},{259,387}..., dimensions={0}, use_global_device_ids=true | all-gather | bytes 221184 | tf_op jit(solution)/shard_map/all_gather | solution.py:38
  111.1 20.3 %all_to_all.26.error_ref = bf16[16,4,16,576]{3,2,1,0:T(8,128)(2,1)S(1)} all-to-all(bf16[16,4,16,576]{3,2,1,0:T(8,128)(2,1)S(1)} %broadcast_in_dim.28), channel_id=1, replica_groups=mesh['zh'=4,'zm'=2,'zb'=2,'xh'=2,'y'=4,'xl'=2,'core'=2] {'zb','xh','y'}, dimensions={0} | all-to-all | bytes 2359296 | tf_op jit(solution)/shard_map/all_to_all | solution.py:19
  131.4 1.0 shard_map.105
  133.1 8.0 %all-to-all-start.4 = ((bf16[4,64,512]{2,1,0:T(8,128)(2,1)}), bf16[4,64,512]{2,1,0:T(8,128)(2,1)S(1)}, u32[]{:S(2)}, u32[]{:S(2)}) async-start(bf16[4,64,512]{2,1,0:T(8,128)(2,1)} %bitcast.27), calls=%async_computation.4 | async-start | bytes 524288 | tf_op jit(solution)/shard_map/all_to_all | solution.py:19
  141.1 1.8 %shard_map.107 = bf16[576,1280]{1,0:T(8,128)(2,1)} custom-call(s32[1]{0:T(128)} %bitcast.source_ref, bf16[16,4,16,576]{3,2,1,0:T(8,128)(2,1)S(1)} %all_to_all.26.error_ref, bf16[256,512]{1,0:T(8,128)(2,1)S(1)} %all_gather.29.codes_ref), custom_call_target="tpu_custom_call" | custom-call | flops 377487360 | bytes 3000000 | tf_op jit(solution)/shard_map/pallas_call | solution.py:125
  142.9 3.4 %all-to-all-done.4 = bf16[4,64,512]{2,1,0:T(8,128)(2,1)S(1)} async-done(((bf16[4,64,512]{2,1,0:T(8,128)(2,1)}), bf16[4,64,512]{2,1,0:T(8,128)(2,1)S(1)}, u32[]{:S(2)}, u32[]{:S(2)}) %all-to-all-start.4) | async-done | bytes 262176 | tf_op jit(solution)/shard_map/all_to_all | solution.py:19
  146.3 6.4 %collective-permute-start = (bf16[64,256]{1,0:T(8,128)(2,1)S(1)}, bf16[64,256]{1,0:T(8,128)(2,1)S(1)}, u32[]{:S(2)}, u32[]{:S(2)}) collective-permute-start(bf16[64,256]{1,0:T(8,128)(2,1)S(1)} %slice.71), channel_id=1, source_target_pairs={{0,384},{128,256},{256,128},{384,0},{1,385},{129,257},{257,129},{3... | collective-permute-start | bytes 98312 | tf_op jit(solution)/shard_map/ppermute | solution.py:32
  153.4 1.6 collective-permute-done
  155.0 7.6 %all_gather.35.grad_ref = bf16[256,512]{1,0:T(8,128)(2,1)S(1)} all-gather(bf16[64,512]{1,0:T(8,128)(2,1)S(1)} %fusion.2), channel_id=1, replica_groups=mesh['zh'=4,'zm'=2,'zb'=2,'xh'=2,'y'=4,'xl'=2,'core'=2] {'xl','core'}, dimensions={0}, use_global_device_ids=true | all-gather | bytes 327680 | tf_op jit(solution)/shard_map/all_gather | solution.py:207
  162.6 1.2 shard_map.106
  (49 shorter events, 2.8 us)
Async XLA Ops:
  0.6 25.2 %copy-start.3 = (bf16[512,576]{0,1:T(8,128)(2,1)S(1)}, bf16[512,576]{0,1:T(8,128)(2,1)}, u32[]{:S(2)}) copy-start(bf16[512,576]{0,1:T(8,128)(2,1)} %param.9) | copy-start | bytes 1769476
  1.4 36.5 %copy-start.10 = (s32[512,256]{1,0:T(8,128)S(1)}, s32[512,256]{1,0:T(8,128)}, u32[]{:S(2)}) copy-start(s32[512,256]{1,0:T(8,128)} %param.11) | copy-start | bytes 1572868
  1.4 36.5 %copy-start.13 = (f32[512]{0:T(512)S(1)}, f32[512]{0:T(512)}, u32[]{:S(2)}) copy-start(f32[512]{0:T(512)} %param.10) | copy-start | bytes 6148
  26.9 29.2 %copy-start = (bf16[1280,576]{0,1:T(8,128)(2,1)S(1)}, bf16[1280,576]{0,1:T(8,128)(2,1)}, u32[]{:S(2)}) copy-start(bf16[1280,576]{0,1:T(8,128)(2,1)} %param.12) | copy-start | bytes 4423684
  26.9 10.9 %all-to-all-start.1 = ((bf16[4,64,512]{2,1,0:T(8,128)(2,1)}), bf16[4,64,512]{2,1,0:T(8,128)(2,1)S(1)}, u32[]{:S(2)}, u32[]{:S(2)}) async-start(bf16[4,64,512]{2,1,0:T(8,128)(2,1)} %bitcast.4), calls=%async_computation.1 | async-start | bytes 524288 | tf_op jit(solution)/shard_map/all_to_all | solution.py:19
  57.1 1.1 copy-start.1
  58.2 24.9 %all-to-all-start.2 = ((bf16[16,4,16,576]{3,2,1,0:T(8,128)(2,1)}), bf16[16,4,16,576]{3,2,1,0:T(8,128)(2,1)S(1)}, u32[]{:S(2)}, u32[]{:S(2)}) async-start(bf16[16,4,16,576]{3,2,1,0:T(8,128)(2,1)} %copy-done.1), calls=%async_computation.2 | async-start | bytes 2621440 | tf_op jit(solution)/shard_map/all_to_all | solution.py:19
  61.9 21.3 %copy-start.12 = (bf16[8,576]{1,0:T(8,128)(2,1)S(1)}, bf16[8,576]{1,0:T(8,128)(2,1)}, u32[]{:S(2)}) copy-start(bf16[8,576]{1,0:T(8,128)(2,1)} %param.8) | copy-start | bytes 27652
  90.4 20.0 %copy-start.4 = (bf16[2,4,16,576]{3,2,1,0:T(8,128)(2,1)}, bf16[2,4,16,576]{3,2,1,0:T(8,128)(2,1)S(1)}, u32[]{:S(2)}) copy-start(bf16[2,4,16,576]{3,2,1,0:T(8,128)(2,1)S(1)} %all_gather.30) | copy-start | bytes 442372
  100.8 9.6 %copy-start.6 = (bf16[8,16,576]{2,1,0:T(8,128)(2,1)}, bf16[8,16,576]{2,1,0:T(8,128)(2,1)S(1)}, u32[]{:S(2)}) copy-start(bf16[8,16,576]{2,1,0:T(8,128)(2,1)S(1)} %all-gather.1) | copy-start | bytes 442372
  110.3 0.7 copy-start.8
  132.4 0.7 copy-start.2
  133.1 13.1 %all-to-all-start.4 = ((bf16[4,64,512]{2,1,0:T(8,128)(2,1)}), bf16[4,64,512]{2,1,0:T(8,128)(2,1)S(1)}, u32[]{:S(2)}, u32[]{:S(2)}) async-start(bf16[4,64,512]{2,1,0:T(8,128)(2,1)} %bitcast.27), calls=%async_computation.4 | async-start | bytes 524288 | tf_op jit(solution)/shard_map/all_to_all | solution.py:19
  141.1 11.6 %copy-start.5 = (bf16[2,4,16,576]{3,2,1,0:T(8,128)(2,1)S(1)}, bf16[2,4,16,576]{3,2,1,0:T(8,128)(2,1)}, u32[]{:S(2)}) copy-start(bf16[2,4,16,576]{3,2,1,0:T(8,128)(2,1)} %copy-done.4) | copy-start | bytes 442372
  141.1 11.6 %copy-start.7 = (bf16[8,16,576]{2,1,0:T(8,128)(2,1)S(1)}, bf16[8,16,576]{2,1,0:T(8,128)(2,1)}, u32[]{:S(2)}) copy-start(bf16[8,16,576]{2,1,0:T(8,128)(2,1)} %copy-done.6) | copy-start | bytes 442372
  141.1 11.7 %copy-start.9 = (bf16[8,16,576]{2,1,0:T(8,128)(2,1)S(1)}, bf16[8,16,576]{2,1,0:T(8,128)(2,1)}, u32[]{:S(2)}) copy-start(bf16[8,16,576]{2,1,0:T(8,128)(2,1)} %copy-done.8) | copy-start | bytes 442372
  142.9 12.1 %copy-start.11 = (f32[64,512]{1,0:T(8,128)S(1)}, f32[64,512]{1,0:T(8,128)}, u32[]{:S(2)}) copy-start(f32[64,512]{1,0:T(8,128)} %get-tuple-element.33) | copy-start | bytes 393220
  146.3 8.7 %collective-permute-start = (bf16[64,256]{1,0:T(8,128)(2,1)S(1)}, bf16[64,256]{1,0:T(8,128)(2,1)S(1)}, u32[]{:S(2)}, u32[]{:S(2)}) collective-permute-start(bf16[64,256]{1,0:T(8,128)(2,1)S(1)} %slice.71), channel_id=1, source_target_pairs={{0,384},{128,256},{256,128},{384,0},{1,385},{129,257},{257,129},{3... | collective-permute-start | bytes 98312 | tf_op jit(solution)/shard_map/ppermute | solution.py:32

commit v5 on v4

--- a/solution.py
+++ b/solution.py
@@ -32,8 +32,7 @@
     return lax.ppermute(piece, "zh", [(s, LAYERS - 1 - s) for s in range(LAYERS)])
 
 
-def both_of(piece, pairs):
-    layer = lax.axis_index("zh")
+def both_of(piece, pairs, layer):
     second = sum((layer == pair[1]).astype(jnp.int32) for pair in pairs)
     return lax.all_gather(piece, "zh", axis=0, axis_index_groups=pairs), 1 - second
 
@@ -157,7 +156,7 @@
     pre = jnp.sum(exchange(pre_part, FEAT).astype(F32), axis=0) + enc_bias[None, :]
     code_q = (mask_q * pre).astype(BF)
     low, high = code_q[:, :span], code_q[:, span:]
-    received = pick(*both_of(jnp.where(first, high, low), MIRRORED))
+    received = pick(*both_of(jnp.where(first, high, low), MIRRORED, source[0]))
     both_q = jnp.concatenate([jnp.where(first, low, high), received], axis=1)
     codes = lax.all_gather(both_q, FEAT, axis=0, tiled=True)
 
@@ -170,8 +169,8 @@
         sum_kernel, array((LAYERS, zm * rows, width), F32), tokens * LAYERS * width, 1400000,
         exchange(pieces, NEAR),
     ).reshape(block)
-    sums, targets = lax.optimization_barrier((sums, mlp_targets))
     layer, place = lax.axis_index("zh"), lax.axis_index("zm")
+    sums, targets, layer, place = lax.optimization_barrier((sums, mlp_targets, layer, place))
     mine = jnp.arange(LAYERS)[:, None] == layer
     mine = (mine & (jnp.arange(zm)[None, :] == place))[:, :, None, None]
     part = (sums - jnp.where(mine, targets.astype(F32)[None, None], 0.0)).astype(BF)
@@ -183,7 +182,7 @@
     arrived = [(near_pair, 1 - place)]
     part = jnp.sum(near_pair.astype(F32), axis=0).astype(BF)
     for pairs in (MIRRORED, ADJACENT):
-        pair, other = both_of(part, pairs)
+        pair, other = both_of(part, pairs, layer)
         arrived.append((pair, other))
         part = jnp.sum(pair.astype(F32), axis=0).astype(BF)
     error = part
@@ -195,7 +194,8 @@
     )
     terms = exchange(terms.reshape(parts, quarter, feats), FEAT)
     terms_q = jnp.sum(terms.astype(F32), axis=0)
-    terms_q, sums, arrived = lax.optimization_barrier((terms_q, sums, arrived))
+    late = (terms_q, sums, arrived, error, codes)
+    terms_q, sums, arrived, error, codes = lax.optimization_barrier(late)
     recon_rows = own_rows(sums)
     for pair, other in arrived:
         recon_rows += own_rows(pick(pair, other).reshape(block)).astype(F32)

time: 164 us -> 165 us (level)
    all_to_all x3, waiting for transfers between devices: 28.9 us -> 30.8 us  [exchange(): return lax.all_to_all(pieces, axes, 0, 0, tiled=True)]
  transfers between devices with their start and end apart: 4 -> 4, of which waited for: 4 -> 3; matrix products, arithmetic and copies ran while one was open for 0% -> 1% of each run, Pallas kernels for 1% -> 1%
where the time goes in v5:
time: 165 us; the launch traced here: 164 us
  blocking collectives  95.6 us (58%)
  waiting for transfers between devices  30.8 us (19%)
  starting transfers between devices  23.9 us (14%)
  Pallas kernels  6.18 us (4%)
  local copies, waits for them, and re-layouts  3.35 us (2%)
  other arithmetic  2.02 us (1%)
    all_to_all x2, blocking collectives, exchange(): return lax.all_to_all(pieces, axes, 0, 0, tiled=True)  44.7 us
    all_to_all x3, waiting for transfers between devices, exchange(): return lax.all_to_all(pieces, axes, 0, 0, tiled=True)  30.8 us
    all_gather x3, blocking collectives, both_of(): lax.all_gather(piece, 'zh', axis=0, axis_index_groups=pairs)  29.9 us
    all_to_all x3, starting transfers between devices, exchange(): return lax.all_to_all(pieces, axes, 0, 0, tiled=True)  17.6 us
    all_gather x1, blocking collectives, body(): codes = lax.all_gather(both_q, FEAT, axis=0, tiled=True)  7.26 us
    all_gather x1, blocking collectives, body(): lax.all_gather(part.reshape(LAYERS, zm * rows, width), 'zm', axis=0)  7.03 us
    all_gather x1, blocking collectives, body(): lax.all_gather((mask_q * grad_q).astype(BF), FEAT, axis=0, tiled=True)  6.78 us
    ppermute x1, starting transfers between devices, mirror(): lax.ppermute(piece, 'zh', [(s, LAYERS - 1 - s) for s in range(LAYERS)])  6.36 us
  transfers between devices with their start and end apart: 4, of which 3 were waited for; matrix products, arithmetic and copies ran while one was open for 1% of the time, Pallas kernels for 1%

profile of v5, /device:TPU:1, one launch (start us, length us, event | category | flops | bytes accessed | tf_op | source)
XLA Modules:
  0.0 164.3 jit_solution(2721082254824888733)
XLA Ops:
  0.6 0.8 broadcast_in_dim.17
  1.5 24.4 %all_to_all.25 = bf16[32,8,576]{2,1,0:T(8,128)(2,1)S(1)} all-to-all(bf16[32,8,576]{2,1,0:T(8,128)(2,1)S(1)} %broadcast_in_dim.17), channel_id=1, replica_groups=mesh['zh'=4,'zm'=2,'zb'=2,'xh'=2,'y'=4,'xl'=2,'core'=2] {'zb','xh','y','..., dimensions={0} | all-to-all | bytes 589824 | tf_op jit(solution)/shard_map/all_to_all | solution.py:19
  25.9 1.1 shard_map.102
  26.9 5.8 %all-to-all-start.1 = ((bf16[4,64,512]{2,1,0:T(8,128)(2,1)}), bf16[4,64,512]{2,1,0:T(8,128)(2,1)S(1)}, u32[]{:S(2)}, u32[]{:S(2)}) async-start(bf16[4,64,512]{2,1,0:T(8,128)(2,1)} %bitcast.4), calls=%async_computation.1 | async-start | bytes 524288 | tf_op jit(solution)/shard_map/all_to_all | solution.py:19
  33.4 4.5 %all-to-all-done.1 = bf16[4,64,512]{2,1,0:T(8,128)(2,1)S(1)} async-done(((bf16[4,64,512]{2,1,0:T(8,128)(2,1)}), bf16[4,64,512]{2,1,0:T(8,128)(2,1)S(1)}, u32[]{:S(2)}, u32[]{:S(2)}) %all-to-all-start.1) | async-done | bytes 262176 | tf_op jit(solution)/shard_map/all_to_all | solution.py:19
  37.9 0.9 multiply_convert_fusion
  38.8 10.0 %all-gather = bf16[128,256]{1,0:T(8,128)(2,1)S(1)} all-gather(bf16[64,256]{1,0:T(8,128)(2,1)S(1)} %get-tuple-element.39), channel_id=2, replica_groups={{0,384},{128,256},{1,385},{129,257},{2,386},{130,258},{3,387},{131,259}..., dimensions={0}, use_global_device_ids=true | all-gather | bytes 98304 | tf_op jit(solution)/shard_map/all_gather | solution.py:37
  48.8 7.3 %all_gather.29.codes_ref = bf16[256,512]{1,0:T(8,128)(2,1)S(1)} all-gather(bf16[64,512]{1,0:T(8,128)(2,1)S(1)} %pad_maximum_fusion), channel_id=1, replica_groups=mesh['zh'=4,'zm'=2,'zb'=2,'xh'=2,'y'=4,'xl'=2,'core'=2] {'xl','core'}, dimensions={0}, use_global_device_ids=true | all-gather | bytes 327680 | tf_op jit(solution)/shard_map/all_gather | solution.py:161
  56.1 1.0 shard_map.103
  57.1 1.0 copy-done.1
  58.2 3.7 %all-to-all-start.2 = ((bf16[16,4,16,576]{3,2,1,0:T(8,128)(2,1)}), bf16[16,4,16,576]{3,2,1,0:T(8,128)(2,1)S(1)}, u32[]{:S(2)}, u32[]{:S(2)}) async-start(bf16[16,4,16,576]{3,2,1,0:T(8,128)(2,1)} %copy-done.1), calls=%async_computation.2 | async-start | bytes 2621440 | tf_op jit(solution)/shard_map/all_to_all | solution.py:19
  61.9 21.1 %all-to-all-done.2.pieces_ref = bf16[16,4,16,576]{3,2,1,0:T(8,128)(2,1)S(1)} async-done(((bf16[16,4,16,576]{3,2,1,0:T(8,128)(2,1)}), bf16[16,4,16,576]{3,2,1,0:T(8,128)(2,1)S(1)}, u32[]{:S(2)}, u32[]{:S(2)}) %all-to-all-start.2) | async-done | bytes 1179680 | tf_op jit(solution)/shard_map/all_to_all | solution.py:19
  83.5 7.0 %all_gather.30 = bf16[2,4,16,576]{3,2,1,0:T(8,128)(2,1)S(1)} all-gather(bf16[1,4,16,576]{3,2,1,0:T(8,128)(2,1)S(1)} %fusion.3), channel_id=1, replica_groups=mesh['zh'=4,'zm'=2,'zb'=2,'xh'=2,'y'=4,'xl'=2,'core'=2] {'zm'}, dimensions={0}, use_global_device_ids=true | all-gather | bytes 221184 | tf_op jit(solution)/shard_map/all_gather | solution.py:181
  90.5 10.4 %all-gather.1 = bf16[8,16,576]{2,1,0:T(8,128)(2,1)S(1)} all-gather(bf16[4,16,576]{2,1,0:T(8,128)(2,1)S(1)} %reduce_sum.55), channel_id=3, replica_groups={{0,384},{128,256},{1,385},{129,257},{2,386},{130,258},{3,387},{131,259}..., dimensions={0}, use_global_device_ids=true | all-gather | bytes 221184 | tf_op jit(solution)/shard_map/all_gather | solution.py:37
  101.0 9.5 %all-gather.2 = bf16[8,16,576]{2,1,0:T(8,128)(2,1)S(1)} all-gather(bf16[4,16,576]{2,1,0:T(8,128)(2,1)S(1)} %reduce_sum.56), channel_id=4, replica_groups={{0,128},{256,384},{1,129},{257,385},{2,130},{258,386},{3,131},{259,387}..., dimensions={0}, use_global_device_ids=true | all-gather | bytes 221184 | tf_op jit(solution)/shard_map/all_gather | solution.py:37
  111.3 20.3 %all_to_all.26.error_ref = bf16[16,4,16,576]{3,2,1,0:T(8,128)(2,1)S(1)} all-to-all(bf16[16,4,16,576]{3,2,1,0:T(8,128)(2,1)S(1)} %broadcast_in_dim.28), channel_id=1, replica_groups=mesh['zh'=4,'zm'=2,'zb'=2,'xh'=2,'y'=4,'xl'=2,'core'=2] {'zb','xh','y'}, dimensions={0} | all-to-all | bytes 2359296 | tf_op jit(solution)/shard_map/all_to_all | solution.py:19
  131.5 1.0 shard_map.105
  133.2 8.1 %all-to-all-start.4 = ((bf16[4,64,512]{2,1,0:T(8,128)(2,1)}), bf16[4,64,512]{2,1,0:T(8,128)(2,1)S(1)}, u32[]{:S(2)}, u32[]{:S(2)}) async-start(bf16[4,64,512]{2,1,0:T(8,128)(2,1)} %bitcast.27), calls=%async_computation.4 | async-start | bytes 524288 | tf_op jit(solution)/shard_map/all_to_all | solution.py:19
  141.3 5.2 %all-to-all-done.4 = bf16[4,64,512]{2,1,0:T(8,128)(2,1)S(1)} async-done(((bf16[4,64,512]{2,1,0:T(8,128)(2,1)}), bf16[4,64,512]{2,1,0:T(8,128)(2,1)S(1)}, u32[]{:S(2)}, u32[]{:S(2)}) %all-to-all-start.4) | async-done | bytes 262176 | tf_op jit(solution)/shard_map/all_to_all | solution.py:19
  146.6 6.4 %collective-permute-start = (bf16[64,256]{1,0:T(8,128)(2,1)S(1)}, bf16[64,256]{1,0:T(8,128)(2,1)S(1)}, u32[]{:S(2)}, u32[]{:S(2)}) collective-permute-start(bf16[64,256]{1,0:T(8,128)(2,1)S(1)} %slice.71), channel_id=1, source_target_pairs={{0,384},{128,256},{256,128},{384,0},{1,385},{129,257},{257,129},{3... | collective-permute-start | bytes 98312 | tf_op jit(solution)/shard_map/ppermute | solution.py:32
  152.9 0.9 select_bitcast_fusion.2
  154.6 1.8 %shard_map.107 = bf16[576,1280]{1,0:T(8,128)(2,1)} custom-call(s32[1]{0:T(128)} %bitcast.source_ref, bf16[16,4,16,576]{3,2,1,0:T(8,128)(2,1)S(1)} %all_to_all.26.error_ref, bf16[256,512]{1,0:T(8,128)(2,1)S(1)} %all_gather.29.codes_ref), custom_call_target="tpu_custom_call" | custom-call | flops 377487360 | bytes 3000000 | tf_op jit(solution)/shard_map/pallas_call | solution.py:124
  156.4 6.8 %all_gather.35.grad_ref = bf16[256,512]{1,0:T(8,128)(2,1)S(1)} all-gather(bf16[64,512]{1,0:T(8,128)(2,1)S(1)} %fusion.2), channel_id=1, replica_groups=mesh['zh'=4,'zm'=2,'zb'=2,'xh'=2,'y'=4,'xl'=2,'core'=2] {'xl','core'}, dimensions={0}, use_global_device_ids=true | all-gather | bytes 327680 | tf_op jit(solution)/shard_map/all_gather | solution.py:207
  163.2 1.2 shard_map.106
  (47 shorter events, 2.8 us)
Async XLA Ops:
  0.6 25.2 %copy-start.3 = (bf16[512,576]{0,1:T(8,128)(2,1)S(1)}, bf16[512,576]{0,1:T(8,128)(2,1)}, u32[]{:S(2)}) copy-start(bf16[512,576]{0,1:T(8,128)(2,1)} %param.9) | copy-start | bytes 1769476
  1.4 36.5 %copy-start.9 = (s32[512,256]{1,0:T(8,128)S(1)}, s32[512,256]{1,0:T(8,128)}, u32[]{:S(2)}) copy-start(s32[512,256]{1,0:T(8,128)} %param.11) | copy-start | bytes 1572868
  1.4 36.5 %copy-start.12 = (f32[512]{0:T(512)S(1)}, f32[512]{0:T(512)}, u32[]{:S(2)}) copy-start(f32[512]{0:T(512)} %param.10) | copy-start | bytes 6148
  26.9 29.2 %copy-start = (bf16[1280,576]{0,1:T(8,128)(2,1)S(1)}, bf16[1280,576]{0,1:T(8,128)(2,1)}, u32[]{:S(2)}) copy-start(bf16[1280,576]{0,1:T(8,128)(2,1)} %param.12) | copy-start | bytes 4423684
  26.9 10.9 %all-to-all-start.1 = ((bf16[4,64,512]{2,1,0:T(8,128)(2,1)}), bf16[4,64,512]{2,1,0:T(8,128)(2,1)S(1)}, u32[]{:S(2)}, u32[]{:S(2)}) async-start(bf16[4,64,512]{2,1,0:T(8,128)(2,1)} %bitcast.4), calls=%async_computation.1 | async-start | bytes 524288 | tf_op jit(solution)/shard_map/all_to_all | solution.py:19
  57.1 1.1 copy-start.1
  58.2 24.9 %all-to-all-start.2 = ((bf16[16,4,16,576]{3,2,1,0:T(8,128)(2,1)}), bf16[16,4,16,576]{3,2,1,0:T(8,128)(2,1)S(1)}, u32[]{:S(2)}, u32[]{:S(2)}) async-start(bf16[16,4,16,576]{3,2,1,0:T(8,128)(2,1)} %copy-done.1), calls=%async_computation.2 | async-start | bytes 2621440 | tf_op jit(solution)/shard_map/all_to_all | solution.py:19
  61.9 21.3 %copy-start.11 = (bf16[8,576]{1,0:T(8,128)(2,1)S(1)}, bf16[8,576]{1,0:T(8,128)(2,1)}, u32[]{:S(2)}) copy-start(bf16[8,576]{1,0:T(8,128)(2,1)} %param.8) | copy-start | bytes 27652
  90.5 20.0 %copy-start.4 = (bf16[2,4,16,576]{3,2,1,0:T(8,128)(2,1)}, bf16[2,4,16,576]{3,2,1,0:T(8,128)(2,1)S(1)}, u32[]{:S(2)}) copy-start(bf16[2,4,16,576]{3,2,1,0:T(8,128)(2,1)S(1)} %all_gather.30) | copy-start | bytes 442372
  100.9 9.6 %copy-start.5 = (bf16[8,16,576]{2,1,0:T(8,128)(2,1)}, bf16[8,16,576]{2,1,0:T(8,128)(2,1)S(1)}, u32[]{:S(2)}) copy-start(bf16[8,16,576]{2,1,0:T(8,128)(2,1)S(1)} %all-gather.1) | copy-start | bytes 442372
  110.4 0.7 copy-start.7
  132.5 0.7 copy-start.2
  133.2 20.7 %copy-start.6 = (bf16[8,16,576]{2,1,0:T(8,128)(2,1)S(1)}, bf16[8,16,576]{2,1,0:T(8,128)(2,1)}, u32[]{:S(2)}) copy-start(bf16[8,16,576]{2,1,0:T(8,128)(2,1)} %copy-done.5) | copy-start | bytes 442372
  133.2 20.7 %copy-start.8 = (bf16[8,16,576]{2,1,0:T(8,128)(2,1)S(1)}, bf16[8,16,576]{2,1,0:T(8,128)(2,1)}, u32[]{:S(2)}) copy-start(bf16[8,16,576]{2,1,0:T(8,128)(2,1)} %copy-done.7) | copy-start | bytes 442372
  133.2 13.3 %all-to-all-start.4 = ((bf16[4,64,512]{2,1,0:T(8,128)(2,1)}), bf16[4,64,512]{2,1,0:T(8,128)(2,1)S(1)}, u32[]{:S(2)}, u32[]{:S(2)}) async-start(bf16[4,64,512]{2,1,0:T(8,128)(2,1)} %bitcast.27), calls=%async_computation.4 | async-start | bytes 524288 | tf_op jit(solution)/shard_map/all_to_all | solution.py:19
  146.6 9.8 %collective-permute-start = (bf16[64,256]{1,0:T(8,128)(2,1)S(1)}, bf16[64,256]{1,0:T(8,128)(2,1)S(1)}, u32[]{:S(2)}, u32[]{:S(2)}) collective-permute-start(bf16[64,256]{1,0:T(8,128)(2,1)S(1)} %slice.71), channel_id=1, source_target_pairs={{0,384},{128,256},{256,128},{384,0},{1,385},{129,257},{257,129},{3... | collective-permute-start | bytes 98312 | tf_op jit(solution)/shard_map/ppermute | solution.py:32
  154.6 1.8 %copy-start.10 = (f32[64,512]{1,0:T(8,128)S(1)}, f32[64,512]{1,0:T(8,128)}, u32[]{:S(2)}) copy-start(f32[64,512]{1,0:T(8,128)} %get-tuple-element.41) | copy-start | bytes 393220

commit v6 on v4

--- a/solution.py
+++ b/solution.py
@@ -26,10 +26,6 @@
 
 MIRRORED = [[0, 3], [1, 2]]
 ADJACENT = [[0, 1], [2, 3]]
-
-
-def mirror(piece):
-    return lax.ppermute(piece, "zh", [(s, LAYERS - 1 - s) for s in range(LAYERS)])
 
 
 def both_of(piece, pairs):
@@ -193,13 +189,13 @@
         terms_kernel, array((tokens, feats)), 8 * 2 * tokens * span * width, 3000000,
         source, error, dec,
     )
+    terms, sums, arrived = lax.optimization_barrier((terms, sums, arrived))
     terms = exchange(terms.reshape(parts, quarter, feats), FEAT)
     terms_q = jnp.sum(terms.astype(F32), axis=0)
-    terms_q, sums, arrived = lax.optimization_barrier((terms_q, sums, arrived))
     recon_rows = own_rows(sums)
     for pair, other in arrived:
         recon_rows += own_rows(pick(pair, other).reshape(block)).astype(F32)
-    returned = mirror(terms_q[:, span:].astype(BF)).astype(F32)
+    returned = pick(*both_of(terms_q[:, span:].astype(BF), MIRRORED)).astype(F32)
     own = terms_q[:, :span]
     grad_q = jnp.concatenate(
         [jnp.where(first, own, returned), jnp.where(first, returned, own)], axis=1

time: 164 us -> 165 us (level)
  waiting for transfers between devices: 30.5 us -> 44.7 us
  blocking collectives: 96.4 us -> 83.6 us
  starting transfers between devices: 23.8 us -> 20.3 us
  other arithmetic: 1.08 us -> 3 us
    all_to_all x2 -> x1, blocking collectives: 44.7 us -> 24.4 us  [exchange(): return lax.all_to_all(pieces, axes, 0, 0, tiled=True)]
    all_to_all x3 -> x4, waiting for transfers between devices: 28.9 us -> 44.7 us  [exchange(): return lax.all_to_all(pieces, axes, 0, 0, tiled=True)]
    all_gather x3 -> x4, blocking collectives: 29.9 us -> 37.3 us  [both_of(): lax.all_gather(piece, 'zh', axis=0, axis_index_groups=pairs)]
    ppermute x1 -> x0, starting transfers between devices: 6.37 us -> none  [mirror(): lax.ppermute(piece, 'zh', [(s, LAYERS - 1 - s) for s in range(LAYERS)])]
    all_to_all x3 -> x4, starting transfers between devices: 17.4 us -> 20.3 us  [exchange(): return lax.all_to_all(pieces, axes, 0, 0, tiled=True)]
    select_n x3, other arithmetic: 0.06 us -> 1.98 us  [pick(): return jnp.where(place == 0, pair[0], pair[1])]
  transfers between devices with their start and end apart: 4 -> 4, of which waited for: 4 -> 4; matrix products, arithmetic and copies ran while one was open for 0% -> 2% of each run, Pallas kernels for 1% -> 1%
where the time goes in v6:
time: 165 us; the launch traced here: 164 us
  blocking collectives  83.6 us (51%)
  waiting for transfers between devices  44.7 us (27%)
  starting transfers between devices  20.3 us (12%)
  Pallas kernels  6.19 us (4%)
  local copies, waits for them, and re-layouts  3.8 us (2%)
  other arithmetic  3 us (2%)
    all_to_all x4, waiting for transfers between devices, exchange(): return lax.all_to_all(pieces, axes, 0, 0, tiled=True)  44.7 us
    all_gather x4, blocking collectives, both_of(): lax.all_gather(piece, 'zh', axis=0, axis_index_groups=pairs)  37.3 us
    all_to_all x1, blocking collectives, exchange(): return lax.all_to_all(pieces, axes, 0, 0, tiled=True)  24.4 us
    all_to_all x4, starting transfers between devices, exchange(): return lax.all_to_all(pieces, axes, 0, 0, tiled=True)  20.3 us
    all_gather x1, blocking collectives, body(): lax.all_gather((mask_q * grad_q).astype(BF), FEAT, axis=0, tiled=True)  7.65 us
    all_gather x1, blocking collectives, body(): codes = lax.all_gather(both_q, FEAT, axis=0, tiled=True)  7.26 us
    all_gather x1, blocking collectives, body(): lax.all_gather(part.reshape(LAYERS, zm * rows, width), 'zm', axis=0)  7.03 us
    pallas_call x6, Pallas kernels, call(): pl.pallas_call(kernel, out_shape=shapes, in_specs=[pl.BlockSpec(memory_sp...  6.19 us
  transfers between devices with their start and end apart: 4, of which 4 were waited for; matrix products, arithmetic and copies ran while one was open for 2% of the time, Pallas kernels for 1%

profile of v6, /device:TPU:1, one launch (start us, length us, event | category | flops | bytes accessed | tf_op | source)
XLA Modules:
  0.0 164.0 jit_solution(5982505090336632062)
XLA Ops:
  1.5 24.4 %all_to_all.25 = bf16[32,8,576]{2,1,0:T(8,128)(2,1)S(1)} all-to-all(bf16[32,8,576]{2,1,0:T(8,128)(2,1)S(1)} %broadcast_in_dim.17), channel_id=1, replica_groups=mesh['zh'=4,'zm'=2,'zb'=2,'xh'=2,'y'=4,'xl'=2,'core'=2] {'zb','xh','y','..., dimensions={0} | all-to-all | bytes 589824 | tf_op jit(solution)/shard_map/all_to_all | solution.py:19
  25.9 1.1 shard_map.102
  26.9 5.8 %all-to-all-start.1 = ((bf16[4,64,512]{2,1,0:T(8,128)(2,1)}), bf16[4,64,512]{2,1,0:T(8,128)(2,1)S(1)}, u32[]{:S(2)}, u32[]{:S(2)}) async-start(bf16[4,64,512]{2,1,0:T(8,128)(2,1)} %bitcast.4), calls=%async_computation.1 | async-start | bytes 524288 | tf_op jit(solution)/shard_map/all_to_all | solution.py:19
  33.4 4.5 %all-to-all-done.1 = bf16[4,64,512]{2,1,0:T(8,128)(2,1)S(1)} async-done(((bf16[4,64,512]{2,1,0:T(8,128)(2,1)}), bf16[4,64,512]{2,1,0:T(8,128)(2,1)S(1)}, u32[]{:S(2)}, u32[]{:S(2)}) %all-to-all-start.1) | async-done | bytes 262176 | tf_op jit(solution)/shard_map/all_to_all | solution.py:19
  38.8 10.0 %all-gather = bf16[128,256]{1,0:T(8,128)(2,1)S(1)} all-gather(bf16[64,256]{1,0:T(8,128)(2,1)S(1)} %get-tuple-element.31), channel_id=2, replica_groups={{0,384},{128,256},{1,385},{129,257},{2,386},{130,258},{3,387},{131,259}..., dimensions={0}, use_global_device_ids=true | all-gather | bytes 98304 | tf_op jit(solution)/shard_map/all_gather | solution.py:34
  48.8 7.3 %all_gather.35.codes_ref = bf16[256,512]{1,0:T(8,128)(2,1)S(1)} all-gather(bf16[64,512]{1,0:T(8,128)(2,1)S(1)} %pad_maximum_fusion), channel_id=1, replica_groups=mesh['zh'=4,'zm'=2,'zb'=2,'xh'=2,'y'=4,'xl'=2,'core'=2] {'xl','core'}, dimensions={0}, use_global_device_ids=true | all-gather | bytes 327680 | tf_op jit(solution)/shard_map/all_gather | solution.py:158
  56.1 1.0 shard_map.103
  57.1 1.0 copy-done.1
  58.2 3.7 %all-to-all-start.2 = ((bf16[16,4,16,576]{3,2,1,0:T(8,128)(2,1)}), bf16[16,4,16,576]{3,2,1,0:T(8,128)(2,1)S(1)}, u32[]{:S(2)}, u32[]{:S(2)}) async-start(bf16[16,4,16,576]{3,2,1,0:T(8,128)(2,1)} %copy-done.1), calls=%async_computation.2 | async-start | bytes 2621440 | tf_op jit(solution)/shard_map/all_to_all | solution.py:19
  62.0 21.0 %all-to-all-done.2.pieces_ref = bf16[16,4,16,576]{3,2,1,0:T(8,128)(2,1)S(1)} async-done(((bf16[16,4,16,576]{3,2,1,0:T(8,128)(2,1)}), bf16[16,4,16,576]{3,2,1,0:T(8,128)(2,1)S(1)}, u32[]{:S(2)}, u32[]{:S(2)}) %all-to-all-start.2) | async-done | bytes 1179680 | tf_op jit(solution)/shard_map/all_to_all | solution.py:19
  83.3 7.0 %all_gather.36 = bf16[2,4,16,576]{3,2,1,0:T(8,128)(2,1)S(1)} all-gather(bf16[1,4,16,576]{3,2,1,0:T(8,128)(2,1)S(1)} %fusion.3), channel_id=1, replica_groups=mesh['zh'=4,'zm'=2,'zb'=2,'xh'=2,'y'=4,'xl'=2,'core'=2] {'zm'}, dimensions={0}, use_global_device_ids=true | all-gather | bytes 221184 | tf_op jit(solution)/shard_map/all_gather | solution.py:178
  90.4 10.4 %all-gather.1 = bf16[8,16,576]{2,1,0:T(8,128)(2,1)S(1)} all-gather(bf16[4,16,576]{2,1,0:T(8,128)(2,1)S(1)} %reduce_sum.55), channel_id=3, replica_groups={{0,384},{128,256},{1,385},{129,257},{2,386},{130,258},{3,387},{131,259}..., dimensions={0}, use_global_device_ids=true | all-gather | bytes 221184 | tf_op jit(solution)/shard_map/all_gather | solution.py:34
  100.9 9.4 %all-gather.2 = bf16[8,16,576]{2,1,0:T(8,128)(2,1)S(1)} all-gather(bf16[4,16,576]{2,1,0:T(8,128)(2,1)S(1)} %reduce_sum.56), channel_id=4, replica_groups={{0,128},{256,384},{1,129},{257,385},{2,130},{258,386},{3,131},{259,387}..., dimensions={0}, use_global_device_ids=true | all-gather | bytes 221184 | tf_op jit(solution)/shard_map/all_gather | solution.py:34
  110.3 1.2 broadcast_in_dim.28
  111.6 3.7 %all-to-all-start.3 = ((bf16[16,4,16,576]{3,2,1,0:T(8,128)(2,1)}), bf16[16,4,16,576]{3,2,1,0:T(8,128)(2,1)S(1)}, u32[]{:S(2)}, u32[]{:S(2)}) async-start(bf16[16,4,16,576]{3,2,1,0:T(8,128)(2,1)} %broadcast_in_dim.28), calls=%async_computation.3 | async-start | bytes 2621440 | tf_op jit(solution)/shard_map/all_to_all | solution.py:19
  115.3 18.4 %all-to-all-done.3.error_ref = bf16[16,4,16,576]{3,2,1,0:T(8,128)(2,1)S(1)} async-done(((bf16[16,4,16,576]{3,2,1,0:T(8,128)(2,1)}), bf16[16,4,16,576]{3,2,1,0:T(8,128)(2,1)S(1)}, u32[]{:S(2)}, u32[]{:S(2)}) %all-to-all-start.3) | async-done | bytes 1179680 | tf_op jit(solution)/shard_map/all_to_all | solution.py:19
  133.6 1.0 shard_map.105
  135.4 7.1 %all-to-all-start.4 = ((bf16[4,64,512]{2,1,0:T(8,128)(2,1)}), bf16[4,64,512]{2,1,0:T(8,128)(2,1)S(1)}, u32[]{:S(2)}, u32[]{:S(2)}) async-start(bf16[4,64,512]{2,1,0:T(8,128)(2,1)} %bitcast.27), calls=%async_computation.4 | async-start | bytes 524288 | tf_op jit(solution)/shard_map/all_to_all | solution.py:19
  142.5 1.0 select_bitcast_fusion
  143.5 0.9 select_bitcast_fusion.2
  144.5 1.8 %shard_map.107 = bf16[576,1280]{1,0:T(8,128)(2,1)} custom-call(s32[1]{0:T(128)} %bitcast.source_ref, bf16[16,4,16,576]{3,2,1,0:T(8,128)(2,1)S(1)} %all-to-all-done.3.error_ref, bf16[256,512]{1,0:T(8,128)(2,1)S(1)} %all_gather.35.codes_ref), custom_call_target="tpu_custom_call" | custom-call | flops 377487360 | bytes 3000000 | tf_op jit(solution)/shard_map/pallas_call | solution.py:121
  147.7 7.4 %all-gather.3 = bf16[128,256]{1,0:T(8,128)(2,1)S(1)} all-gather(bf16[64,256]{1,0:T(8,128)(2,1)S(1)} %slice.94), channel_id=5, replica_groups={{0,384},{128,256},{1,385},{129,257},{2,386},{130,258},{3,387},{131,259}..., dimensions={0}, use_global_device_ids=true | all-gather | bytes 98304 | tf_op jit(solution)/shard_map/all_gather | solution.py:34
  155.2 7.6 %all_gather.43.grad_ref = bf16[256,512]{1,0:T(8,128)(2,1)S(1)} all-gather(bf16[64,512]{1,0:T(8,128)(2,1)S(1)} %fusion.2), channel_id=1, replica_groups=mesh['zh'=4,'zm'=2,'zb'=2,'xh'=2,'y'=4,'xl'=2,'core'=2] {'xl','core'}, dimensions={0}, use_global_device_ids=true | all-gather | bytes 327680 | tf_op jit(solution)/shard_map/all_gather | solution.py:203
  162.8 1.2 shard_map.106
  (43 shorter events, 4.4 us)
Async XLA Ops:
  0.6 25.2 %copy-start.3 = (bf16[512,576]{0,1:T(8,128)(2,1)S(1)}, bf16[512,576]{0,1:T(8,128)(2,1)}, u32[]{:S(2)}) copy-start(bf16[512,576]{0,1:T(8,128)(2,1)} %param.9) | copy-start | bytes 1769476
  1.4 36.5 %copy-start.7 = (s32[512,256]{1,0:T(8,128)S(1)}, s32[512,256]{1,0:T(8,128)}, u32[]{:S(2)}) copy-start(s32[512,256]{1,0:T(8,128)} %param.11) | copy-start | bytes 1572868
  1.4 36.5 %copy-start.10 = (f32[512]{0:T(512)S(1)}, f32[512]{0:T(512)}, u32[]{:S(2)}) copy-start(f32[512]{0:T(512)} %param.10) | copy-start | bytes 6148
  26.9 29.2 %copy-start = (bf16[1280,576]{0,1:T(8,128)(2,1)S(1)}, bf16[1280,576]{0,1:T(8,128)(2,1)}, u32[]{:S(2)}) copy-start(bf16[1280,576]{0,1:T(8,128)(2,1)} %param.12) | copy-start | bytes 4423684
  26.9 10.9 %all-to-all-start.1 = ((bf16[4,64,512]{2,1,0:T(8,128)(2,1)}), bf16[4,64,512]{2,1,0:T(8,128)(2,1)S(1)}, u32[]{:S(2)}, u32[]{:S(2)}) async-start(bf16[4,64,512]{2,1,0:T(8,128)(2,1)} %bitcast.4), calls=%async_computation.1 | async-start | bytes 524288 | tf_op jit(solution)/shard_map/all_to_all | solution.py:19
  57.1 1.1 copy-start.1
  58.2 24.9 %all-to-all-start.2 = ((bf16[16,4,16,576]{3,2,1,0:T(8,128)(2,1)}), bf16[16,4,16,576]{3,2,1,0:T(8,128)(2,1)S(1)}, u32[]{:S(2)}, u32[]{:S(2)}) async-start(bf16[16,4,16,576]{3,2,1,0:T(8,128)(2,1)} %copy-done.1), calls=%async_computation.2 | async-start | bytes 2621440 | tf_op jit(solution)/shard_map/all_to_all | solution.py:19
  61.9 21.3 %copy-start.9 = (bf16[8,576]{1,0:T(8,128)(2,1)S(1)}, bf16[8,576]{1,0:T(8,128)(2,1)}, u32[]{:S(2)}) copy-start(bf16[8,576]{1,0:T(8,128)(2,1)} %param.8) | copy-start | bytes 27652
  90.4 21.2 %copy-start.4 = (bf16[2,4,16,576]{3,2,1,0:T(8,128)(2,1)}, bf16[2,4,16,576]{3,2,1,0:T(8,128)(2,1)S(1)}, u32[]{:S(2)}) copy-start(bf16[2,4,16,576]{3,2,1,0:T(8,128)(2,1)S(1)} %all_gather.36) | copy-start | bytes 442372
  100.8 10.7 %copy-start.5 = (bf16[8,16,576]{2,1,0:T(8,128)(2,1)}, bf16[8,16,576]{2,1,0:T(8,128)(2,1)S(1)}, u32[]{:S(2)}) copy-start(bf16[8,16,576]{2,1,0:T(8,128)(2,1)S(1)} %all-gather.1) | copy-start | bytes 442372
  110.3 1.3 copy-start.6
  111.6 22.1 %all-to-all-start.3 = ((bf16[16,4,16,576]{3,2,1,0:T(8,128)(2,1)}), bf16[16,4,16,576]{3,2,1,0:T(8,128)(2,1)S(1)}, u32[]{:S(2)}, u32[]{:S(2)}) async-start(bf16[16,4,16,576]{3,2,1,0:T(8,128)(2,1)} %broadcast_in_dim.28), calls=%async_computation.3 | async-start | bytes 2621440 | tf_op jit(solution)/shard_map/all_to_all | solution.py:19
  134.6 0.7 copy-start.2
  135.4 12.3 %all-to-all-start.4 = ((bf16[4,64,512]{2,1,0:T(8,128)(2,1)}), bf16[4,64,512]{2,1,0:T(8,128)(2,1)S(1)}, u32[]{:S(2)}, u32[]{:S(2)}) async-start(bf16[4,64,512]{2,1,0:T(8,128)(2,1)} %bitcast.27), calls=%async_computation.4 | async-start | bytes 524288 | tf_op jit(solution)/shard_map/all_to_all | solution.py:19
  144.4 10.7 %copy-start.8 = (f32[64,512]{1,0:T(8,128)S(1)}, f32[64,512]{1,0:T(8,128)}, u32[]{:S(2)}) copy-start(f32[64,512]{1,0:T(8,128)} %get-tuple-element.33) | copy-start | bytes 393220
